TPU v7x, 32 devices: a whole 2x2x4 slice. The times are simulated.
32 devices in a mesh: dp: 8 (over z, y), mp: 4 (over x, core).
Axes of the slice: x: 2, y: 2, z: 4, core: 2. Of those that a mesh axis runs over, the one named last changes fastest.
Arguments:
- block_input: bfloat16 [8192, 1024], P(('dp', 'mp')), may hold values from -6 to 6
- latent_table: bfloat16 [256, 1024], replicated, may hold values from -6 to 6
- latent_segments: int32 [8, 1024], P('dp'), may hold values from 0 to 15, as said below
- input_segments: int32 [8, 1024], P('dp'), may hold values from 0 to 15, as said below
- ln_gain: float32 [4, 1024], replicated, may hold values from 0.1 to 1.9
- ln_bias: float32 [4, 1024], replicated, may hold values from -2.5 to 2.5
- cross_query: bfloat16 [1024, 1024], P(None, 'mp'), may hold values from -0.1875 to 0.1875
- cross_key: bfloat16 [1024, 1024], P(None, 'mp'), may hold values from -0.1875 to 0.1875
- cross_value: bfloat16 [1024, 1024], P(None, 'mp'), may hold values from -0.1875 to 0.1875
- cross_out: bfloat16 [1024, 1024], P(None, 'mp'), may hold values from -1 to 1
- self_query: bfloat16 [1024, 1024], P(None, 'mp'), may hold values from -0.1875 to 0.1875
- self_key: bfloat16 [1024, 1024], P(None, 'mp'), may hold values from -0.1875 to 0.1875
- self_value: bfloat16 [1024, 1024], P(None, 'mp'), may hold values from -0.1875 to 0.1875
- self_out: bfloat16 [1024, 1024], P(None, 'mp'), may hold values from -1 to 1
- up_proj: bfloat16 [1024, 4096], P(None, 'mp'), may hold values from -0.1875 to 0.1875
- down_proj: bfloat16 [1024, 4096], P(None, 'mp'), may hold values from -0.125 to 0.125
- out_grad: bfloat16 [8192, 1024], P(('dp', 'mp')), may hold values from -6 to 6
Outputs:
- block_output: float32 [8192, 1024], P(('dp', 'mp'))
- input_grad: float32 [8192, 1024], P(('dp', 'mp'))
- table_grad: float32 [256, 1024], replicated
- ln_gain_grad: float32 [4, 1024], replicated
- ln_bias_grad: float32 [3, 1024], replicated
- mlp_bias_grad: float32 [1024], replicated
- cross_query_grad: float32 [1024, 1024], P('dp', 'mp')
- cross_key_grad: float32 [1024, 1024], P('dp', 'mp')
- cross_value_grad: float32 [1024, 1024], P('dp', 'mp')
- cross_out_grad: float32 [1024, 1024], P('dp', 'mp')
- self_query_grad: float32 [1024, 1024], P('dp', 'mp')
- self_key_grad: float32 [1024, 1024], P('dp', 'mp')
- self_value_grad: float32 [1024, 1024], P('dp', 'mp')
- self_out_grad: float32 [1024, 1024], P('dp', 'mp')
- up_proj_grad: float32 [1024, 4096], P('dp', 'mp')
- down_proj_grad: float32 [1024, 4096], P('dp', 'mp')
Inputs may be any that keep to these rules, and one draw needn't show every extreme that they name: `latent_segments`: in each packed row the ids never fall, every id from 0 to 15 occurs, no image has more than 256 latent rows, and one image has exactly 256. `input_segments`: in each packed row the ids never fall, every id from 0 to 15 occurs, no image has more than 256 input rows, and one image has exactly 256.
All inputs are finite; a program needn't handle non-finite values.
Results may differ from a plain program's by a relative error of at most 0.028.
Values may be sent and summed in bfloat16 or wider, within the bound.
No kernel may reach another device: no remote copies, remote signals or barrier semaphores. Data moves between devices by JAX's collectives and lax.ppermute only.
A program may use at most 128 MiB of HBM per device.

v0:
```python
import jax
import jax.numpy as jnp
from jax import lax
from jax.sharding import PartitionSpec as P

HEAD = 128


norm_eps = 1e-05
masked_score = -1e30
highest = lax.Precision.HIGHEST
gelu_coeff = 0.7978845608028654


def layer_norm(values, gain, offset):
    average = jnp.mean(values, axis=-1, keepdims=True)
    centred = values - average
    spread = jnp.mean(centred * centred, axis=-1, keepdims=True)
    return centred * lax.rsqrt(spread + norm_eps) * gain + offset


def gelu_tanh(values):
    return (
        0.5 * values * (1.0 + jnp.tanh(gelu_coeff * (values + 0.044715 * values * values * values)))
    )


def project(left, right):
    return jnp.dot(left, right, preferred_element_type=jnp.float32)


def project_back(left, right):
    return lax.dot_general(
        left, right, (((1,), (1,)), ((), ())), preferred_element_type=jnp.float32
    )


def outer_sum(left, right):
    return lax.dot_general(
        left, right, (((0,), (0,)), ((), ())), preferred_element_type=jnp.float32
    )


def rows_of(source, row_start, row_count):
    return lax.dynamic_slice_in_dim(source, row_start, row_count, 0)


def gather_rows(local_rows):
    return lax.all_gather(local_rows, "mp", axis=0, tiled=True)


def gather_grads(local_rows):
    return lax.all_gather(local_rows, "mp", axis=0, tiled=True)


def send_rows(mixed_rows, weight, local_count):

    def row_term(row_start, row_count):
        return project_back(rows_of(mixed_rows, row_start, row_count), weight)

    return lax.psum_scatter(
        row_term(jnp.int32(0), local_count * lax.axis_size("mp")),
        "mp",
        scatter_dimension=0,
        tiled=True,
    )


def send_grads(grad_pairs, local_count):

    def row_term(row_start, row_count):
        partial_sum = project_back(
            rows_of(grad_pairs[0][0], row_start, row_count), grad_pairs[0][1]
        )
        for grad_rows, weight in grad_pairs[1:]:
            partial_sum = partial_sum + project_back(
                rows_of(grad_rows, row_start, row_count), weight
            )
        return partial_sum

    return lax.psum_scatter(
        row_term(jnp.int32(0), local_count * lax.axis_size("mp")),
        "mp",
        scatter_dimension=0,
        tiled=True,
    )


def split_heads(rows):
    return rows.reshape(rows.shape[0], rows.shape[1] // HEAD, HEAD)


def block_size():
    return 512


def masked_scores(query_block, key_heads, query_ids, key_ids):
    scores = jnp.einsum(
        "qhd,khd->hqk", query_block, key_heads, preferred_element_type=jnp.float32
    ) * HEAD ** (-0.5)
    allowed = query_ids[:, None] == key_ids[None, :]
    return jnp.where(allowed[None], scores, masked_score)


def attention(queries, key_rows, values, query_ids, key_ids):
    row_total = queries.shape[0]
    local_width = queries.shape[1]
    block_rows = block_size()
    key_heads = split_heads(key_rows)
    value_heads = split_heads(values)

    def one_block(block_index):
        row_start = block_index * block_rows
        query_block = split_heads(rows_of(queries, row_start, block_rows))
        scores = masked_scores(
            query_block, key_heads, rows_of(query_ids, row_start, block_rows), key_ids
        )
        row_peak = jnp.max(scores, axis=-1, keepdims=True)
        log_total = row_peak + jnp.log(jnp.sum(jnp.exp(scores - row_peak), axis=-1, keepdims=True))
        weights = jnp.exp(scores - log_total).astype(jnp.bfloat16)
        mixed_heads = jnp.einsum(
            "hqk,khd->qhd", weights, value_heads, preferred_element_type=jnp.float32
        )
        return (mixed_heads.reshape(block_rows, local_width), log_total)

    mixed_blocks, log_blocks = lax.map(one_block, jnp.arange(row_total // block_rows))
    return (mixed_blocks.reshape(row_total, local_width).astype(jnp.bfloat16), log_blocks)


def attention_back(queries, key_rows, values, log_blocks, grad_mixed, query_ids, key_ids):
    row_total = queries.shape[0]
    local_width = queries.shape[1]
    block_rows = block_size()
    key_heads = split_heads(key_rows)
    value_heads = split_heads(values)
    score_scale = HEAD ** (-0.5)

    def one_block(running, block_item):
        block_index, log_total = block_item
        key_grad, value_grad = running
        row_start = block_index * block_rows
        query_block = split_heads(rows_of(queries, row_start, block_rows))
        grad_block = split_heads(rows_of(grad_mixed, row_start, block_rows))
        scores = masked_scores(
            query_block, key_heads, rows_of(query_ids, row_start, block_rows), key_ids
        )
        row_probs = jnp.exp(scores - log_total)
        grad_probs = jnp.einsum(
            "qhd,khd->hqk", grad_block, value_heads, preferred_element_type=jnp.float32
        )
        row_inner = jnp.sum(row_probs * grad_probs, axis=-1, keepdims=True)
        grad_scores = (row_probs * (grad_probs - row_inner)).astype(jnp.bfloat16)
        query_grad = (
            jnp.einsum("hqk,khd->qhd", grad_scores, key_heads, preferred_element_type=jnp.float32)
            * score_scale
        )
        key_grad = (
            key_grad
            + jnp.einsum(
                "hqk,qhd->khd", grad_scores, query_block, preferred_element_type=jnp.float32
            )
            * score_scale
        )
        value_grad = value_grad + jnp.einsum(
            "hqk,qhd->khd",
            row_probs.astype(jnp.bfloat16),
            grad_block,
            preferred_element_type=jnp.float32,
        )
        return ((key_grad, value_grad), query_grad.reshape(block_rows, local_width))

    zero_grads = jnp.zeros(key_heads.shape, jnp.float32)
    (key_grad, value_grad), query_blocks = lax.scan(
        one_block, (zero_grads, zero_grads), (jnp.arange(row_total // block_rows), log_blocks)
    )
    key_count = key_rows.shape[0]
    return (
        query_blocks.reshape(row_total, local_width).astype(jnp.bfloat16),
        key_grad.reshape(key_count, local_width).astype(jnp.bfloat16),
        value_grad.reshape(key_count, local_width).astype(jnp.bfloat16),
    )


def body(
    block_input,
    latent_table,
    latent_segments,
    input_segments,
    ln_gain,
    ln_bias,
    cross_query,
    cross_key,
    cross_value,
    cross_out,
    self_query,
    self_key,
    self_value,
    self_out,
    up_proj,
    down_proj,
    out_grad,
):
    local_count = block_input.shape[0]
    member = lax.axis_index("mp")
    latent_ids = latent_segments[0]
    input_ids = input_segments[0]
    own_ids = rows_of(latent_ids, member * local_count, local_count)
    earlier = jnp.sum(
        (latent_ids[None, :] < own_ids[:, None]).astype(jnp.int32), axis=1, dtype=jnp.int32
    )
    slot_index = member * local_count + jnp.arange(local_count, dtype=jnp.int32) - earlier
    table_pick = (
        slot_index[:, None] == jnp.arange(latent_table.shape[0], dtype=jnp.int32)[None, :]
    ).astype(jnp.bfloat16)
    start_rows = project(table_pick, latent_table)
    normed_latent = layer_norm(start_rows, ln_gain[0], ln_bias[0]).astype(jnp.bfloat16)
    input_rows = block_input.astype(jnp.float32)
    normed_input = layer_norm(input_rows, ln_gain[1], ln_bias[1]).astype(jnp.bfloat16)
    whole_latent = gather_rows(normed_latent)
    whole_input = gather_rows(normed_input)
    cross_queries = project(whole_latent, cross_query).astype(jnp.bfloat16)
    cross_keys = project(whole_input, cross_key).astype(jnp.bfloat16)
    cross_values = project(whole_input, cross_value).astype(jnp.bfloat16)
    cross_mixed, cross_logs = attention(
        cross_queries, cross_keys, cross_values, latent_ids, input_ids
    )
    after_cross = start_rows + send_rows(cross_mixed, cross_out, local_count)
    normed_self = layer_norm(after_cross, ln_gain[2], ln_bias[2]).astype(jnp.bfloat16)
    whole_self = gather_rows(normed_self)
    self_queries = project(whole_self, self_query).astype(jnp.bfloat16)
    self_keys = project(whole_self, self_key).astype(jnp.bfloat16)
    self_values = project(whole_self, self_value).astype(jnp.bfloat16)
    self_mixed, self_logs = attention(self_queries, self_keys, self_values, latent_ids, latent_ids)
    after_self = after_cross + send_rows(self_mixed, self_out, local_count)
    normed_mlp = layer_norm(after_self, ln_gain[3], ln_bias[3]).astype(jnp.bfloat16)
    whole_mlp = gather_rows(normed_mlp)
    hidden = project(whole_mlp, up_proj)
    active = gelu_tanh(hidden).astype(jnp.bfloat16)
    block_output = after_self + send_rows(active, down_proj, local_count)
    grad_last = out_grad.astype(jnp.float32)
    whole_grad = gather_grads(out_grad)
    down_grad = outer_sum(whole_grad, active)
    grad_active = project(whole_grad, down_proj)
    gelu_value, gelu_pull = jax.vjp(gelu_tanh, hidden)
    grad_hidden = gelu_pull(grad_active)[0].astype(jnp.bfloat16)
    up_grad = outer_sum(whole_mlp, grad_hidden)
    grad_normed = send_grads(((grad_hidden, up_proj),), local_count)
    norm_value, norm_pull = jax.vjp(layer_norm, after_self, ln_gain[3], ln_bias[3])
    grad_rows, gain_mlp, bias_mlp = norm_pull(grad_normed)
    grad_self = grad_last + grad_rows
    whole_grad = gather_grads(grad_self.astype(jnp.bfloat16))
    self_out_grad = outer_sum(whole_grad, self_mixed)
    grad_mixed = project(whole_grad, self_out).astype(jnp.bfloat16)
    query_grads, key_grads, value_grads = attention_back(
        self_queries, self_keys, self_values, self_logs, grad_mixed, latent_ids, latent_ids
    )
    self_query_grad = outer_sum(whole_self, query_grads)
    self_key_grad = outer_sum(whole_self, key_grads)
    self_value_grad = outer_sum(whole_self, value_grads)
    grad_normed = send_grads(
        ((query_grads, self_query), (key_grads, self_key), (value_grads, self_value)), local_count
    )
    norm_value, norm_pull = jax.vjp(layer_norm, after_cross, ln_gain[2], ln_bias[2])
    grad_rows, gain_self, bias_self = norm_pull(grad_normed)
    grad_cross = grad_self + grad_rows
    whole_grad = gather_grads(grad_cross.astype(jnp.bfloat16))
    cross_out_grad = outer_sum(whole_grad, cross_mixed)
    grad_mixed = project(whole_grad, cross_out).astype(jnp.bfloat16)
    query_grads, key_grads, value_grads = attention_back(
        cross_queries, cross_keys, cross_values, cross_logs, grad_mixed, latent_ids, input_ids
    )
    cross_query_grad = outer_sum(whole_latent, query_grads)
    cross_key_grad = outer_sum(whole_input, key_grads)
    cross_value_grad = outer_sum(whole_input, value_grads)
    grad_latent = send_grads(((query_grads, cross_query),), local_count)
    grad_input = send_grads(((key_grads, cross_key), (value_grads, cross_value)), local_count)
    norm_value, norm_pull = jax.vjp(layer_norm, start_rows, ln_gain[0], ln_bias[0])
    grad_rows, gain_latent, bias_latent = norm_pull(grad_latent)
    grad_start = grad_cross + grad_rows
    norm_value, norm_pull = jax.vjp(layer_norm, input_rows, ln_gain[1], ln_bias[1])
    grad_input_rows, gain_input, bias_input = norm_pull(grad_input)
    table_part = lax.dot_general(
        table_pick.astype(jnp.float32),
        grad_start,
        (((0,), (0,)), ((), ())),
        precision=highest,
        preferred_element_type=jnp.float32,
    )
    gain_part = jnp.stack([gain_latent, gain_input, gain_self, gain_mlp])
    bias_part = jnp.stack([bias_latent, bias_input, bias_self, bias_mlp])
    table_grad, ln_gain_grad, offset_grads = lax.psum(
        (table_part, gain_part, bias_part), ("dp", "mp")
    )
    every_summed = (
        lax.psum_scatter(cross_query_grad, "dp", scatter_dimension=0, tiled=True),
        lax.psum_scatter(cross_key_grad, "dp", scatter_dimension=0, tiled=True),
        lax.psum_scatter(cross_value_grad, "dp", scatter_dimension=0, tiled=True),
        lax.psum_scatter(cross_out_grad, "dp", scatter_dimension=0, tiled=True),
        lax.psum_scatter(self_query_grad, "dp", scatter_dimension=0, tiled=True),
        lax.psum_scatter(self_key_grad, "dp", scatter_dimension=0, tiled=True),
        lax.psum_scatter(self_value_grad, "dp", scatter_dimension=0, tiled=True),
        lax.psum_scatter(self_out_grad, "dp", scatter_dimension=0, tiled=True),
        lax.psum_scatter(up_grad, "dp", scatter_dimension=0, tiled=True),
        lax.psum_scatter(down_grad, "dp", scatter_dimension=0, tiled=True),
    )
    attention_summed = every_summed[:8]
    up_summed = every_summed[8]
    down_summed = every_summed[9]
    return (
        block_output,
        grad_input_rows,
        table_grad,
        ln_gain_grad,
        offset_grads[:3],
        offset_grads[3],
        attention_summed[0],
        attention_summed[1],
        attention_summed[2],
        attention_summed[3],
        attention_summed[4],
        attention_summed[5],
        attention_summed[6],
        attention_summed[7],
        up_summed,
        down_summed,
    )


def solution(mesh):
    placed = (
        P(("dp", "mp"), None),
        P(),
        P("dp", None),
        P("dp", None),
        P(),
        P(),
        P(None, "mp"),
        P(None, "mp"),
        P(None, "mp"),
        P(None, "mp"),
        P(None, "mp"),
        P(None, "mp"),
        P(None, "mp"),
        P(None, "mp"),
        P(None, "mp"),
        P(None, "mp"),
        P(("dp", "mp"), None),
    )
    return jax.shard_map(
        body,
        mesh=mesh,
        in_specs=placed,
        out_specs=(
            P(("dp", "mp"), None),
            P(("dp", "mp"), None),
            P(),
            P(),
            P(),
            P(),
            P("dp", "mp"),
            P("dp", "mp"),
            P("dp", "mp"),
            P("dp", "mp"),
            P("dp", "mp"),
            P("dp", "mp"),
            P("dp", "mp"),
            P("dp", "mp"),
            P("dp", "mp"),
            P("dp", "mp"),
        ),
        check_vma=False,
    )
```

profile of v0, /device:TPU:0, one launch (start us, length us, event | category | flops | bytes accessed | tf_op | source)
XLA Modules:
  0.0 1499.4 jit_solution(2026015541903029730)
XLA Ops:
  19.0 20.8 %all-gather.10.cloned.1.call-done = bf16[1024,1024]{1,0:T(8,128)(2,1)} async-done(((bf16[256,1024]{1,0:T(8,128)(2,1)}), bf16[1024,1024]{1,0:T(8,128)(2,1)}) %all-gather.10.cloned.1.call-update) | async-done | bytes 2097168 | tf_op jit(solution)/shard_map/all_gather | solution.py:49
  39.8 3.2 convolution_convert_fusion.6
  45.1 19.5 %all-gather.8.cloned.1.call-done = bf16[1024,1024]{1,0:T(8,128)(2,1)} async-done(((bf16[256,1024]{1,0:T(8,128)(2,1)}), bf16[1024,1024]{1,0:T(8,128)(2,1)}) %all-gather.8.cloned.1.call-update) | async-done | bytes 2097168 | tf_op jit(solution)/shard_map/all_gather | solution.py:49
  64.6 3.2 convolution_convert_fusion.7
  69.8 3.2 convolution_convert_fusion.5
  73.9 20.1 %while.54 = (s32[]{:T(128)}, bf16[2,512,256]{2,1,0:T(8,128)(2,1)}, f32[2,2,512,1]{2,1,3,0:T(2,128)S(1)}, s32[2]{0:T(128)S(1)}, s32[1024]{0:T(1024)S(1)}, /*index...) while((s32[]{:T(128)}, bf16[2,512,256]{2,1,0:T(8,128)(2,1)}, ...), condition=%wide.region_8.9_spmd, body=%wide.region_5.8_spmd.sunk | while | flops 548928512 | bytes 19966188 | solution.py:126
  93.9 3.9 fusion.87
  97.9 44.6 %reduce-scatter.18.cloned.1.call-done = f32[256,1024]{1,0:T(8,128)} async-done(((f32[1024,1024]{1,0:T(8,128)}), f32[256,1024]{1,0:T(8,128)}) %reduce-scatter.18.cloned.1.call-update) | async-done | bytes 1048592 | tf_op jit(solution)/shard_map/reduce_scatter | solution.py:61
  146.2 22.5 %all-gather.12.cloned.1.call-done = bf16[1024,1024]{1,0:T(8,128)(2,1)} async-done(((bf16[256,1024]{1,0:T(8,128)(2,1)}), bf16[1024,1024]{1,0:T(8,128)(2,1)}) %all-gather.12.cloned.1.call-update) | async-done | bytes 2097168 | tf_op jit(solution)/shard_map/all_gather | solution.py:49
  168.7 2.4 convolution_convert_fusion.3
  171.4 3.2 convolution_convert_fusion.4
  176.7 3.3 convolution_convert_fusion.2
  180.8 14.6 while.55
  195.4 4.0 fusion.88
  200.1 44.0 %reduce-scatter.20.cloned.1.call-done = f32[256,1024]{1,0:T(8,128)} async-done(((f32[1024,1024]{1,0:T(8,128)}), f32[256,1024]{1,0:T(8,128)}) %reduce-scatter.20.cloned.1.call-update) | async-done | bytes 1048592 | tf_op jit(solution)/shard_map/reduce_scatter | solution.py:61
  248.0 20.1 %all-gather.16.cloned.1.call-done = bf16[1024,1024]{1,0:T(8,128)(2,1)} async-done(((bf16[256,1024]{1,0:T(8,128)(2,1)}), bf16[1024,1024]{1,0:T(8,128)(2,1)}) %all-gather.16.cloned.1.call-update) | async-done | bytes 2097168 | tf_op jit(solution)/shard_map/all_gather | solution.py:53
  268.1 6.5 fusion.89
  274.7 18.2 %all-gather.14.cloned.1.call-done = bf16[1024,1024]{1,0:T(8,128)(2,1)} async-done(((bf16[256,1024]{1,0:T(8,128)(2,1)}), bf16[1024,1024]{1,0:T(8,128)(2,1)}) %all-gather.14.cloned.1.call-update) | async-done | bytes 2097168 | tf_op jit(solution)/shard_map/all_gather | solution.py:49
  292.9 8.9 fusion.47
  303.1 4.4 fusion.90
  309.1 6.9 fusion.75
  316.1 36.1 %reduce-scatter.24.cloned.1.call-done = f32[256,1024]{1,0:T(8,128)} async-done(((f32[1024,1024]{1,0:T(8,128)}), f32[256,1024]{1,0:T(8,128)}) %reduce-scatter.24.cloned.1.call-update) | async-done | bytes 1048592 | tf_op jit(solution)/shard_map/reduce_scatter | solution.py:81
  354.5 45.0 %reduce-scatter.22.cloned.1.call-done = f32[256,1024]{1,0:T(8,128)} async-done(((f32[1024,1024]{1,0:T(8,128)}), f32[256,1024]{1,0:T(8,128)}) %reduce-scatter.22.cloned.1.call-update) | async-done | bytes 1048592 | tf_op jit(solution)/shard_map/reduce_scatter | solution.py:61
  399.5 2.9 fusion.79
  402.4 2.4 fusion.64
  407.1 20.4 %all-gather.18.cloned.1.call-done = bf16[1024,1024]{1,0:T(8,128)(2,1)} async-done(((bf16[256,1024]{1,0:T(8,128)(2,1)}), bf16[1024,1024]{1,0:T(8,128)(2,1)}) %all-gather.18.cloned.1.call-update) | async-done | bytes 2097168 | tf_op jit(solution)/shard_map/all_gather | solution.py:53
  427.5 3.2 convolution_convert_fusion.1
  431.6 29.2 %while.56 = (s32[]{:T(128)}, f32[1024,2,128]{0,2,1:T(8,128)S(1)}, f32[1024,2,128]{0,2,1:T(8,128)}, bf16[2,512,256]{2,1,0:T(8,128)(2,1)}, s32[2]{0:T(128)S(1)}, /...) while((s32[]{:T(128)}, f32[1024,2,128]{0,2,1:T(8,128)S(1)}, ...), condition=%wide.region_25.26_spmd.clone, body=%wide.region_23.25_spmd.clone.sunk | while | flops 1360002048 | bytes 51681636 | solution.py:173
  437.2 2.5 fusion.245
  451.1 3.8 fusion.245
  465.4 2.8 add_add_fusion
  468.2 44.6 %reduce-scatter.26.cloned.1.call-done = f32[256,1024]{1,0:T(8,128)} async-done(((f32[1024,1024]{1,0:T(8,128)}), f32[256,1024]{1,0:T(8,128)}) %reduce-scatter.26.cloned.1.call-update) | async-done | bytes 1048592 | tf_op jit(solution)/shard_map/reduce_scatter | solution.py:81
  516.1 2.5 fusion.74
  518.6 7.6 convolution_bitcast_fusion
  528.2 13.2 all-gather.20.cloned.1.call-done
  541.3 3.1 convolution_convert_fusion
  545.3 24.8 %while.57 = (s32[]{:T(128)}, f32[1024,2,128]{0,2,1:T(8,128)S(1)}, f32[1024,2,128]{0,2,1:T(8,128)}, bf16[2,512,256]{2,1,0:T(8,128)(2,1)}, s32[2]{0:T(128)S(1)}, /...) while((s32[]{:T(128)}, f32[1024,2,128]{0,2,1:T(8,128)S(1)}, ...), condition=%wide.region_31.32_spmd.clone, body=%wide.region_29.31_spmd.clone.sunk | while | flops 1360002048 | bytes 43292916 | solution.py:173
  548.9 2.5 fusion.258
  560.7 3.7 fusion.258
  573.7 2.7 convolution_add_fusion
  577.6 2.7 fusion.94
  581.9 6.0 fusion.103
  588.0 3.6 fusion.102
  593.8 2.8 fusion.99
  598.6 3.5 fusion.95
  602.2 3.5 fusion.98
  607.7 3.4 fusion.97
  611.3 22.6 %reduce-scatter.50.cloned.1.call-done = f32[128,1024]{0,1:T(8,128)} async-done(((f32[1024,1024]{0,1:T(8,128)}), f32[128,1024]{0,1:T(8,128)}) %reduce-scatter.50.cloned.1.call-update) | async-done | bytes 524304 | tf_op jit(solution)/shard_map/reduce_scatter | solution.py:304
  635.9 44.6 %reduce-scatter.28.cloned.1.call-done = f32[256,1024]{1,0:T(8,128)} async-done(((f32[1024,1024]{1,0:T(8,128)}), f32[256,1024]{1,0:T(8,128)}) %reduce-scatter.28.cloned.1.call-update) | async-done | bytes 1048592 | tf_op jit(solution)/shard_map/reduce_scatter | solution.py:81
  682.1 45.5 %reduce-scatter.30.cloned.1.call-done = f32[256,1024]{1,0:T(8,128)} async-done(((f32[1024,1024]{1,0:T(8,128)}), f32[256,1024]{1,0:T(8,128)}) %reduce-scatter.30.cloned.1.call-update) | async-done | bytes 1048592 | tf_op jit(solution)/shard_map/reduce_scatter | solution.py:81
  731.0 3.7 fusion.61
  736.6 41.9 %all-reduce = (f32[4,1024]{1,0:T(4,128)}, f32[4,1024]{1,0:T(4,128)S(1)}) all-reduce(f32[4,1024]{1,0:T(4,128)S(1)} %get-tuple-element.636, f32[4,1024]{1,0:T(4,128)S(1)} %get-tuple-element.637), channel_id=1, replica_groups=mesh['dp'=8,'mp'=4] {'dp','mp'}, use_global_device_ids=true, to_apply=%region_43.44 | all-reduce | flops 8192 | bytes 65536 | tf_op jit(solution)/shard_map/psum | solution.py:291
  779.0 2.5 broadcast_add_fusion
  781.6 39.8 %reduce-scatter.48.cloned.1.call-done = f32[128,1024]{1,0:T(8,128)} async-done(((f32[1024,1024]{1,0:T(8,128)}), f32[128,1024]{1,0:T(8,128)}) %reduce-scatter.48.cloned.1.call-update) | async-done | bytes 524304 | tf_op jit(solution)/shard_map/reduce_scatter | solution.py:303
  821.3 67.5 %reduce-scatter.46.cloned.1.call-done = f32[128,256]{1,0:T(8,128)} async-done(((f32[1024,256]{1,0:T(8,128)}), f32[128,256]{1,0:T(8,128)}) %reduce-scatter.46.cloned.1.call-update) | async-done | bytes 131088 | tf_op jit(solution)/shard_map/reduce_scatter | solution.py:302
  888.8 66.4 %reduce-scatter.44.cloned.1.call-done = f32[128,256]{1,0:T(8,128)} async-done(((f32[1024,256]{1,0:T(8,128)}), f32[128,256]{1,0:T(8,128)}) %reduce-scatter.44.cloned.1.call-update) | async-done | bytes 131088 | tf_op jit(solution)/shard_map/reduce_scatter | solution.py:301
  955.2 66.9 %reduce-scatter.40.cloned.1.call-done = f32[128,256]{1,0:T(8,128)} async-done(((f32[1024,256]{1,0:T(8,128)}), f32[128,256]{1,0:T(8,128)}) %reduce-scatter.40.cloned.1.call-update) | async-done | bytes 131088 | tf_op jit(solution)/shard_map/reduce_scatter | solution.py:299
  1022.1 66.2 %reduce-scatter.42.cloned.1.call-done = f32[128,256]{1,0:T(8,128)} async-done(((f32[1024,256]{1,0:T(8,128)}), f32[128,256]{1,0:T(8,128)}) %reduce-scatter.42.cloned.1.call-update) | async-done | bytes 131088 | tf_op jit(solution)/shard_map/reduce_scatter | solution.py:300
  1088.3 66.8 %reduce-scatter.32.cloned.1.call-done = f32[128,256]{1,0:T(8,128)} async-done(((f32[1024,256]{1,0:T(8,128)}), f32[128,256]{1,0:T(8,128)}) %reduce-scatter.32.cloned.1.call-update) | async-done | bytes 131088 | tf_op jit(solution)/shard_map/reduce_scatter | solution.py:295
  1155.1 66.5 %reduce-scatter.38.cloned.1.call-done = f32[128,256]{1,0:T(8,128)} async-done(((f32[1024,256]{1,0:T(8,128)}), f32[128,256]{1,0:T(8,128)}) %reduce-scatter.38.cloned.1.call-update) | async-done | bytes 131088 | tf_op jit(solution)/shard_map/reduce_scatter | solution.py:298
  1221.6 66.9 %reduce-scatter.34.cloned.1.call-done = f32[128,256]{1,0:T(8,128)} async-done(((f32[1024,256]{1,0:T(8,128)}), f32[128,256]{1,0:T(8,128)}) %reduce-scatter.34.cloned.1.call-update) | async-done | bytes 131088 | tf_op jit(solution)/shard_map/reduce_scatter | solution.py:296
  1288.5 66.2 %reduce-scatter.36.cloned.1.call-done = f32[128,256]{1,0:T(8,128)} async-done(((f32[1024,256]{1,0:T(8,128)}), f32[128,256]{1,0:T(8,128)}) %reduce-scatter.36.cloned.1.call-update) | async-done | bytes 131088 | tf_op jit(solution)/shard_map/reduce_scatter | solution.py:297
  1354.7 135.5 %all-reduce.3.cloned.1.call-done = f32[256,1024]{1,0:T(8,128)} async-done(((f32[256,1024]{1,0:T(8,128)}), f32[256,1024]{1,0:T(8,128)}) %all-reduce.3.cloned.1.call-update) | async-done | bytes 1048592 | tf_op jit(solution)/shard_map/psum | solution.py:291
  1490.1 2.3 copy.193
  (361 shorter events, 139.1 us)
Async XLA Ops:
  7.2 285.7 %copy-start = (bf16[1024,1024]{1,0:T(8,128)(2,1)S(1)}, bf16[1024,1024]{1,0:T(8,128)(2,1)}, u32[]{:S(2)}) copy-start(bf16[1024,1024]{1,0:T(8,128)(2,1)} %param.39) | copy-start | bytes 6291460
  7.2 32.6 %all-gather.10.cloned.1.call-start = ((), (), s32[]{:S(2)}) async-start(), calls=%async_computation.18 | async-start | bytes 2621440 | tf_op jit(solution)/shard_map/all_gather | solution.py:49
  8.6 34.5 %copy-start.45 = (f32[256]{0:T(256)}, f32[256]{0:T(256)S(1)}, u32[]{:S(2)}) copy-start(f32[256]{0:T(256)S(1)} %broadcast_multiply_fusion.2) | copy-start | bytes 3076
  10.4 7.1 copy-start.49
  11.3 31.7 %copy-start.43 = (f32[1,1024]{1,0:T(1,128)}, f32[1,1024]{1,0:T(1,128)S(1)}, u32[]{:S(2)}) copy-start(f32[1,1024]{1,0:T(1,128)S(1)} %get-tuple-element.626) | copy-start | bytes 12292
  14.4 50.2 %all-gather.8.cloned.1.call-start = ((), (), s32[]{:S(2)}) async-start(), calls=%async_computation.17 | async-start | bytes 2621440 | tf_op jit(solution)/shard_map/all_gather | solution.py:49
  17.5 125.0 %copy-start.2 = (f32[256,1024]{1,0:T(8,128)}, f32[256,1024]{1,0:T(8,128)S(1)}, u32[]{:S(2)}) copy-start(f32[256,1024]{1,0:T(8,128)S(1)} %get-tuple-element.633) | copy-start | bytes 3145732
  17.6 50.2 %copy-start.47 = (f32[256]{0:T(256)}, f32[256]{0:T(256)S(1)}, u32[]{:S(2)}) copy-start(f32[256]{0:T(256)S(1)} %broadcast_multiply_fusion.3) | copy-start | bytes 3076
  17.8 49.9 %copy-start.57 = (f32[256]{0:T(256)}, f32[256]{0:T(256)S(1)}, u32[]{:S(2)}) copy-start(f32[256]{0:T(256)S(1)} %multiply_reduce_fusion.10) | copy-start | bytes 3076
  17.9 49.9 %copy-start.51 = (f32[256]{0:T(256)}, f32[256]{0:T(256)S(1)}, u32[]{:S(2)}) copy-start(f32[256]{0:T(256)S(1)} %fusion.69) | copy-start | bytes 3076
  18.9 123.6 %reduce-scatter.18.cloned.1.call-start = ((), (), s32[]{:S(2)}) async-start(), calls=%async_computation.19 | async-start | bytes 5242880 | tf_op jit(solution)/shard_map/reduce_scatter | solution.py:61
  45.1 28.7 %copy-start.29 = (s32[1,1024]{1,0:T(1,128)S(1)}, s32[1,1024]{1,0:T(1,128)}, u32[]{:S(2)}) copy-start(s32[1,1024]{1,0:T(1,128)} %param.27) | copy-start | bytes 12292
  45.1 28.7 %copy-start.37 = (s32[1,1024]{1,0:T(1,128)S(1)}, s32[1,1024]{1,0:T(1,128)}, u32[]{:S(2)}) copy-start(s32[1,1024]{1,0:T(1,128)} %param.28) | copy-start | bytes 12292
  97.9 70.9 %all-gather.12.cloned.1.call-start = ((), (), s32[]{:S(2)}) async-start(), calls=%async_computation.20 | async-start | bytes 2621440 | tf_op jit(solution)/shard_map/all_gather | solution.py:49
  146.0 98.1 %reduce-scatter.20.cloned.1.call-start = ((), (), s32[]{:S(2)}) async-start(), calls=%async_computation.21 | async-start | bytes 5242880 | tf_op jit(solution)/shard_map/reduce_scatter | solution.py:61
  171.1 8.8 copy-start.9
  195.4 48.7 %copy-start.5 = (f32[256,1024]{1,0:T(8,128)S(1)}, f32[256,1024]{1,0:T(8,128)}, u32[]{:S(2)}) copy-start(f32[256,1024]{1,0:T(8,128)} %copy-done.4) | copy-start | bytes 3145732
  199.4 68.7 %all-gather.16.cloned.1.call-start = ((), (), s32[]{:S(2)}) async-start(), calls=%async_computation.24 | async-start | bytes 2621440 | tf_op jit(solution)/shard_map/all_gather | solution.py:53
  200.0 92.9 %all-gather.14.cloned.1.call-start = ((), (), s32[]{:S(2)}) async-start(), calls=%async_computation.22 | async-start | bytes 2621440 | tf_op jit(solution)/shard_map/all_gather | solution.py:49
  247.5 104.7 %reduce-scatter.24.cloned.1.call-start = ((), (), s32[]{:S(2)}) async-start(), calls=%async_computation.25 | async-start | bytes 5242880 | tf_op jit(solution)/shard_map/reduce_scatter | solution.py:81
  307.6 91.9 %reduce-scatter.22.cloned.1.call-start = ((), (), s32[]{:S(2)}) async-start(), calls=%async_computation.23 | async-start | bytes 5242880 | tf_op jit(solution)/shard_map/reduce_scatter | solution.py:61
  316.1 36.2 %copy-start.7 = (f32[256,1024]{1,0:T(8,128)S(1)}, f32[256,1024]{1,0:T(8,128)}, u32[]{:S(2)}) copy-start(f32[256,1024]{1,0:T(8,128)} %copy-done.6) | copy-start | bytes 3145732
  316.1 111.5 %all-gather.18.cloned.1.call-start = ((), (), s32[]{:S(2)}) async-start(), calls=%async_computation.26 | async-start | bytes 2621440 | tf_op jit(solution)/shard_map/all_gather | solution.py:53
  402.3 28.4 %copy-start.16 = (f32[256,1024]{1,0:T(8,128)}, f32[256,1024]{1,0:T(8,128)S(1)}, u32[]{:S(2)}) copy-start(f32[256,1024]{1,0:T(8,128)S(1)} %get-tuple-element.610) | copy-start | bytes 3145732
  404.8 108.1 %reduce-scatter.26.cloned.1.call-start = ((), (), s32[]{:S(2)}) async-start(), calls=%async_computation.27 | async-start | bytes 5242880 | tf_op jit(solution)/shard_map/reduce_scatter | solution.py:81
  460.9 4.5 copy-start.20
  468.2 47.9 %copy-start.17 = (f32[256,1024]{1,0:T(8,128)S(1)}, f32[256,1024]{1,0:T(8,128)}, u32[]{:S(2)}) copy-start(f32[256,1024]{1,0:T(8,128)} %copy-done.16) | copy-start | bytes 3145732
  468.2 73.2 %all-gather.20.cloned.1.call-start = ((), (), s32[]{:S(2)}) async-start(), calls=%async_computation.28 | async-start | bytes 2621440 | tf_op jit(solution)/shard_map/all_gather | solution.py:53
  516.1 10.2 copy-start.18
  518.6 115.3 %reduce-scatter.50.cloned.1.call-start = ((), (), s32[]{:S(2)}) async-start(), calls=%async_computation.41 | async-start | bytes 4718592 | tf_op jit(solution)/shard_map/reduce_scatter | solution.py:304
  526.3 15.1 %copy-start.31 = (bf16[1024,256]{1,0:T(8,128)(2,1)S(1)}, bf16[1024,256]{1,0:T(8,128)(2,1)}, u32[]{:S(2)}) copy-start(bf16[1024,256]{1,0:T(8,128)(2,1)} %param.34) | copy-start | bytes 1572868
  526.3 19.0 %copy-start.8 = (bf16[1024,256]{0,1:T(8,128)(2,1)S(1)}, bf16[1024,256]{0,1:T(8,128)(2,1)}, u32[]{:S(2)}) copy-start(bf16[1024,256]{0,1:T(8,128)(2,1)} %convolution_convert_fusion.6) | copy-start | bytes 1572868
  526.3 19.0 %copy-start.15 = (bf16[1024,256]{0,1:T(8,128)(2,1)S(1)}, bf16[1024,256]{0,1:T(8,128)(2,1)}, u32[]{:S(2)}) copy-start(bf16[1024,256]{0,1:T(8,128)(2,1)} %get-tuple-element.1135) | copy-start | bytes 1572868
  526.3 19.0 %copy-start.38 = (s32[1,1024]{1,0:T(1,128)S(1)}, s32[1,1024]{1,0:T(1,128)}, u32[]{:S(2)}) copy-start(s32[1,1024]{1,0:T(1,128)} %param.28) | copy-start | bytes 12292
  526.3 19.0 %copy-start.42 = (f32[2,2,512,1]{2,1,3,0:T(2,128)S(1)}, f32[2,2,512,1]{2,1,3,0:T(2,128)}, u32[]{:S(2)}) copy-start(f32[2,2,512,1]{2,1,3,0:T(2,128)} %copy-done.41) | copy-start | bytes 24580
  526.3 154.2 %reduce-scatter.28.cloned.1.call-start = ((), (), s32[]{:S(2)}) async-start(), calls=%async_computation.29 | async-start | bytes 5242880 | tf_op jit(solution)/shard_map/reduce_scatter | solution.py:81
  570.2 6.2 copy-start.22
  576.4 151.2 %reduce-scatter.30.cloned.1.call-start = ((), (), s32[]{:S(2)}) async-start(), calls=%async_computation.30 | async-start | bytes 5242880 | tf_op jit(solution)/shard_map/reduce_scatter | solution.py:81
  580.3 241.0 %reduce-scatter.48.cloned.1.call-start = ((), (), s32[]{:S(2)}) async-start(), calls=%async_computation.40 | async-start | bytes 4718592 | tf_op jit(solution)/shard_map/reduce_scatter | solution.py:303
  587.9 300.9 %reduce-scatter.46.cloned.1.call-start = ((), (), s32[]{:S(2)}) async-start(), calls=%async_computation.39 | async-start | bytes 1179648 | tf_op jit(solution)/shard_map/reduce_scatter | solution.py:302
  591.6 363.5 %reduce-scatter.44.cloned.1.call-start = ((), (), s32[]{:S(2)}) async-start(), calls=%async_computation.38 | async-start | bytes 1179648 | tf_op jit(solution)/shard_map/reduce_scatter | solution.py:301
  593.8 428.3 %reduce-scatter.40.cloned.1.call-start = ((), (), s32[]{:S(2)}) async-start(), calls=%async_computation.36 | async-start | bytes 1179648 | tf_op jit(solution)/shard_map/reduce_scatter | solution.py:299
  596.7 491.6 %reduce-scatter.42.cloned.1.call-start = ((), (), s32[]{:S(2)}) async-start(), calls=%async_computation.37 | async-start | bytes 1179648 | tf_op jit(solution)/shard_map/reduce_scatter | solution.py:300
  598.6 556.5 %reduce-scatter.32.cloned.1.call-start = ((), (), s32[]{:S(2)}) async-start(), calls=%async_computation.32 | async-start | bytes 1179648 | tf_op jit(solution)/shard_map/reduce_scatter | solution.py:295
  602.2 619.4 %reduce-scatter.38.cloned.1.call-start = ((), (), s32[]{:S(2)}) async-start(), calls=%async_computation.35 | async-start | bytes 1179648 | tf_op jit(solution)/shard_map/reduce_scatter | solution.py:298
  605.8 682.7 %reduce-scatter.34.cloned.1.call-start = ((), (), s32[]{:S(2)}) async-start(), calls=%async_computation.33 | async-start | bytes 1179648 | tf_op jit(solution)/shard_map/reduce_scatter | solution.py:296
  607.6 73.0 %copy-start.14 = (bf16[256,1024]{1,0:T(8,128)(2,1)S(1)}, bf16[256,1024]{1,0:T(8,128)(2,1)}, u32[]{:S(2)}) copy-start(bf16[256,1024]{1,0:T(8,128)(2,1)} %param.25) | copy-start | bytes 1572868
  607.6 73.0 %copy-start.40 = (f32[1,1024]{1,0:T(1,128)S(1)}, f32[1,1024]{1,0:T(1,128)}, u32[]{:S(2)}) copy-start(f32[1,1024]{1,0:T(1,128)} %copy-done.39) | copy-start | bytes 12292
  607.6 73.0 %copy-start.46 = (f32[256]{0:T(256)S(1)}, f32[256]{0:T(256)}, u32[]{:S(2)}) copy-start(f32[256]{0:T(256)} %copy-done.45) | copy-start | bytes 3076
  607.6 120.0 %copy-start.3 = (f32[256,1024]{1,0:T(8,128)S(1)}, f32[256,1024]{1,0:T(8,128)}, u32[]{:S(2)}) copy-start(f32[256,1024]{1,0:T(8,128)} %copy-done.2) | copy-start | bytes 3145732
  607.7 120.0 %copy-start.44 = (f32[1,1024]{1,0:T(1,128)S(1)}, f32[1,1024]{1,0:T(1,128)}, u32[]{:S(2)}) copy-start(f32[1,1024]{1,0:T(1,128)} %copy-done.43) | copy-start | bytes 12292
  607.7 120.0 %copy-start.48 = (f32[256]{0:T(256)S(1)}, f32[256]{0:T(256)}, u32[]{:S(2)}) copy-start(f32[256]{0:T(256)} %copy-done.47) | copy-start | bytes 3076
  607.7 120.0 %copy-start.52 = (f32[256]{0:T(256)S(1)}, f32[256]{0:T(256)}, u32[]{:S(2)}) copy-start(f32[256]{0:T(256)} %copy-done.51) | copy-start | bytes 3076
  607.7 747.0 %reduce-scatter.36.cloned.1.call-start = ((), (), s32[]{:S(2)}) async-start(), calls=%async_computation.34 | async-start | bytes 1179648 | tf_op jit(solution)/shard_map/reduce_scatter | solution.py:297
  611.2 118.1 %copy-start.58 = (f32[256]{0:T(256)S(1)}, f32[256]{0:T(256)}, u32[]{:S(2)}) copy-start(f32[256]{0:T(256)} %copy-done.57) | copy-start | bytes 3076
  611.2 119.7 %copy-start.56 = (f32[256]{0:T(256)S(1)}, f32[256]{0:T(256)}, u32[]{:S(2)}) copy-start(f32[256]{0:T(256)} %copy-done.55) | copy-start | bytes 3076
  611.2 119.7 %copy-start.19 = (bf16[256,1024]{1,0:T(8,128)(2,1)S(1)}, bf16[256,1024]{1,0:T(8,128)(2,1)}, u32[]{:S(2)}) copy-start(bf16[256,1024]{1,0:T(8,128)(2,1)} %param.41) | copy-start | bytes 1572868
  611.2 119.7 %copy-start.60 = (s32[256]{0:T(256)S(1)}, s32[256]{0:T(256)}, u32[]{:S(2)}) copy-start(s32[256]{0:T(256)} %copy-done.59) | copy-start | bytes 3076
  611.2 878.9 %all-reduce.3.cloned.1.call-start = ((), (), s32[]{:S(2)}) async-start(), calls=%async_computation.31 | async-start | bytes 2097152 | tf_op jit(solution)/shard_map/psum | solution.py:291
  729.3 5.5 copy-start.50
  730.9 5.6 copy-start.53
  730.9 5.6 copy-start.54
  731.0 761.5 %copy-start.1 = (bf16[1024,1024]{1,0:T(8,128)(2,1)S(1)}, bf16[1024,1024]{1,0:T(8,128)(2,1)}, u32[]{:S(2)}) copy-start(bf16[1024,1024]{1,0:T(8,128)(2,1)} %param.39) | copy-start | bytes 6291460
  778.4 714.0 %copy-start.61 = (f32[4,1024]{1,0:T(4,128)}, f32[4,1024]{1,0:T(4,128)S(1)}, u32[]{:S(2)}) copy-start(f32[4,1024]{1,0:T(4,128)S(1)} %get-tuple-element.600) | copy-start | bytes 49156
  (32 other events, 72.9 us)
Sparse Core Ops, SparseCore 0:
  14.5 25.2 all-gather.9
  41.9 22.5 all-gather.7
  98.0 44.4 reduce-scatter.17
  146.1 22.5 all-gather.11
  199.6 44.4 reduce-scatter.19
  245.5 22.5 all-gather.15
  270.3 22.5 all-gather.13
  307.7 44.5 reduce-scatter.23
  355.0 44.4 reduce-scatter.21
  404.9 22.5 all-gather.17
  468.3 44.4 reduce-scatter.25
  518.7 22.5 all-gather.19
  545.4 88.4 reduce-scatter.49
  636.3 44.2 reduce-scatter.27
  683.1 44.4 reduce-scatter.29
  731.7 89.6 reduce-scatter.47
  825.5 63.2 reduce-scatter.45
  892.7 62.4 reduce-scatter.43
  959.5 62.5 reduce-scatter.39
  1025.9 62.3 reduce-scatter.41
  1092.6 62.3 reduce-scatter.31
  1159.0 62.5 reduce-scatter.37
  1226.0 62.4 reduce-scatter.33
  1292.3 62.3 reduce-scatter.35
  1361.3 128.8 all-reduce.2
where the time goes:
time: 1510 us; the launch traced here: 1500 us
  waiting for transfers between devices  1170 us (77%)
  matrix products  159 us (11%)
  local copies, waits for them, and re-layouts  53.1 us (4%)
  other arithmetic  51.1 us (3%)
  blocking collectives  41.9 us (3%)
  between operations  15.3 us (1%)
    reduce_scatter x4, waiting for transfers between devices, send_grads(): lax.psum_scatter(row_term(jnp.int32(0), local_count * lax.axis_size('mp')...  171 us
    psum x1, waiting for transfers between devices, body(): lax.psum((table_part, gain_part, bias_part), ('dp', 'mp'))  135 us
    reduce_scatter x3, waiting for transfers between devices, send_rows(): lax.psum_scatter(row_term(jnp.int32(0), local_count * lax.axis_size('mp')...  134 us
    all_gather x4, waiting for transfers between devices, gather_rows(): return lax.all_gather(local_rows, 'mp', axis=0, tiled=True)  81 us
    reduce_scatter x1, waiting for transfers between devices, body(): lax.psum_scatter(self_out_grad, 'dp', scatter_dimension=0, tiled=True)  67.5 us
    reduce_scatter x1, waiting for transfers between devices, body(): lax.psum_scatter(self_query_grad, 'dp', scatter_dimension=0, tiled=True)  66.9 us
    reduce_scatter x1, waiting for transfers between devices, body(): lax.psum_scatter(cross_key_grad, 'dp', scatter_dimension=0, tiled=True)  66.9 us
    reduce_scatter x1, waiting for transfers between devices, body(): lax.psum_scatter(cross_query_grad, 'dp', scatter_dimension=0, tiled=True)  66.8 us
  transfers between devices with their start and end apart: 25, of which 25 were waited for; matrix products, arithmetic and copies ran while one was open for 8% of the time, Pallas kernels for 0%

commit v1 on v0

v1 whole, which is shorter than its diff:
```python
import jax
import jax.numpy as jnp
from jax import lax
from jax.sharding import PartitionSpec as P

HEAD = 128


norm_eps = 1e-05
masked_score = -1e30
highest = lax.Precision.HIGHEST
gelu_coeff = 0.7978845608028654


def layer_norm(values, gain, offset):
    average = jnp.mean(values, axis=-1, keepdims=True)
    centred = values - average
    spread = jnp.mean(centred * centred, axis=-1, keepdims=True)
    return centred * lax.rsqrt(spread + norm_eps) * gain + offset


def gelu_tanh(values):
    return (
        0.5 * values * (1.0 + jnp.tanh(gelu_coeff * (values + 0.044715 * values * values * values)))
    )


def project(left, right):
    return jnp.dot(left, right, preferred_element_type=jnp.float32)


def project_back(left, right):
    return lax.dot_general(
        left, right, (((1,), (1,)), ((), ())), preferred_element_type=jnp.float32
    )


def outer_sum(left, right):
    return lax.dot_general(
        left, right, (((0,), (0,)), ((), ())), preferred_element_type=jnp.float32
    )


def rows_of(source, row_start, row_count):
    return lax.dynamic_slice_in_dim(source, row_start, row_count, 0)


def swap(values, axis, bit):
    return lax.ppermute(values, axis, [(i, i ^ bit) for i in range(lax.axis_size(axis))])


def share_rows(own):
    far = swap(own, "mp", 2)
    near = swap(own, "mp", 1)
    across = swap(far, "mp", 1)
    return jnp.concatenate([own, near, far, across])


def sum_rows(parts):
    count = parts.shape[0] // 4
    own, near, far, across = (parts[i * count : (i + 1) * count] for i in range(4))
    low = jnp.bfloat16
    got_far = swap(across.astype(low), "mp", 1)
    send_far = (far + got_far.astype(jnp.float32)).astype(low)
    got_own = swap(near.astype(low), "mp", 1)
    got_all = swap(send_far, "mp", 2)
    return own + got_own.astype(jnp.float32) + got_all.astype(jnp.float32)


def split_heads(rows):
    return rows.reshape(rows.shape[0], rows.shape[1] // HEAD, HEAD)


def block_size():
    return 512


def masked_scores(query_block, key_heads, query_ids, key_ids):
    scores = jnp.einsum(
        "qhd,khd->hqk", query_block, key_heads, preferred_element_type=jnp.float32
    ) * HEAD ** (-0.5)
    allowed = query_ids[:, None] == key_ids[None, :]
    return jnp.where(allowed[None], scores, masked_score)


def attention(queries, key_rows, values, query_ids, key_ids):
    row_total = queries.shape[0]
    local_width = queries.shape[1]
    block_rows = block_size()
    key_heads = split_heads(key_rows)
    value_heads = split_heads(values)

    def one_block(block_index):
        row_start = block_index * block_rows
        query_block = split_heads(rows_of(queries, row_start, block_rows))
        scores = masked_scores(
            query_block, key_heads, rows_of(query_ids, row_start, block_rows), key_ids
        )
        row_peak = jnp.max(scores, axis=-1, keepdims=True)
        log_total = row_peak + jnp.log(jnp.sum(jnp.exp(scores - row_peak), axis=-1, keepdims=True))
        weights = jnp.exp(scores - log_total).astype(jnp.bfloat16)
        mixed_heads = jnp.einsum(
            "hqk,khd->qhd", weights, value_heads, preferred_element_type=jnp.float32
        )
        return (mixed_heads.reshape(block_rows, local_width), log_total)

    mixed_blocks, log_blocks = lax.map(one_block, jnp.arange(row_total // block_rows))
    return (mixed_blocks.reshape(row_total, local_width).astype(jnp.bfloat16), log_blocks)


def attention_back(queries, key_rows, values, log_blocks, grad_mixed, query_ids, key_ids):
    row_total = queries.shape[0]
    local_width = queries.shape[1]
    block_rows = block_size()
    key_heads = split_heads(key_rows)
    value_heads = split_heads(values)
    score_scale = HEAD ** (-0.5)

    def one_block(running, block_item):
        block_index, log_total = block_item
        key_grad, value_grad = running
        row_start = block_index * block_rows
        query_block = split_heads(rows_of(queries, row_start, block_rows))
        grad_block = split_heads(rows_of(grad_mixed, row_start, block_rows))
        scores = masked_scores(
            query_block, key_heads, rows_of(query_ids, row_start, block_rows), key_ids
        )
        row_probs = jnp.exp(scores - log_total)
        grad_probs = jnp.einsum(
            "qhd,khd->hqk", grad_block, value_heads, preferred_element_type=jnp.float32
        )
        row_inner = jnp.sum(row_probs * grad_probs, axis=-1, keepdims=True)
        grad_scores = (row_probs * (grad_probs - row_inner)).astype(jnp.bfloat16)
        query_grad = (
            jnp.einsum("hqk,khd->qhd", grad_scores, key_heads, preferred_element_type=jnp.float32)
            * score_scale
        )
        key_grad = (
            key_grad
            + jnp.einsum(
                "hqk,qhd->khd", grad_scores, query_block, preferred_element_type=jnp.float32
            )
            * score_scale
        )
        value_grad = value_grad + jnp.einsum(
            "hqk,qhd->khd",
            row_probs.astype(jnp.bfloat16),
            grad_block,
            preferred_element_type=jnp.float32,
        )
        return ((key_grad, value_grad), query_grad.reshape(block_rows, local_width))

    zero_grads = jnp.zeros(key_heads.shape, jnp.float32)
    (key_grad, value_grad), query_blocks = lax.scan(
        one_block, (zero_grads, zero_grads), (jnp.arange(row_total // block_rows), log_blocks)
    )
    key_count = key_rows.shape[0]
    return (
        query_blocks.reshape(row_total, local_width).astype(jnp.bfloat16),
        key_grad.reshape(key_count, local_width).astype(jnp.bfloat16),
        value_grad.reshape(key_count, local_width).astype(jnp.bfloat16),
    )


def body(
    block_input,
    latent_table,
    latent_segments,
    input_segments,
    ln_gain,
    ln_bias,
    cross_query,
    cross_key,
    cross_value,
    cross_out,
    self_query,
    self_key,
    self_value,
    self_out,
    up_proj,
    down_proj,
    out_grad,
):
    low = jnp.bfloat16
    local_count = block_input.shape[0]
    member = lax.axis_index("mp")
    slots = latent_table.shape[0]
    order = [member ^ k for k in range(4)]

    def relative(ids):
        return jnp.concatenate([rows_of(ids, k * local_count, local_count) for k in order])

    row_total = latent_segments.shape[1]
    latent_abs = latent_segments[0]
    latent_ids = relative(latent_abs)
    input_ids = relative(input_segments[0])
    positions = relative(jnp.arange(row_total, dtype=jnp.int32))
    earlier = jnp.sum(
        (latent_abs[None, :] < latent_ids[:, None]).astype(jnp.int32), axis=1, dtype=jnp.int32
    )
    table_pick = (
        (positions - earlier)[:, None] == jnp.arange(slots, dtype=jnp.int32)[None, :]
    ).astype(low)
    own_pick = table_pick[:local_count]
    start_rows = project(own_pick, latent_table)
    table_rows = latent_table.astype(jnp.float32)
    normed_table = layer_norm(table_rows, ln_gain[0], ln_bias[0]).astype(low)
    input_rows = block_input.astype(jnp.float32)
    normed_input = layer_norm(input_rows, ln_gain[1], ln_bias[1]).astype(low)
    whole_input = share_rows(normed_input)
    whole_grad_out = share_rows(out_grad)
    table_queries = project(normed_table, cross_query).astype(low)
    cross_queries = project(table_pick, table_queries).astype(low)
    cross_keys = project(whole_input, cross_key).astype(low)
    cross_values = project(whole_input, cross_value).astype(low)
    cross_mixed, cross_logs = attention(
        cross_queries, cross_keys, cross_values, latent_ids, input_ids
    )
    after_cross = start_rows + sum_rows(project_back(cross_mixed, cross_out))
    normed_self = layer_norm(after_cross, ln_gain[2], ln_bias[2]).astype(low)
    whole_self = share_rows(normed_self)
    self_queries = project(whole_self, self_query).astype(low)
    self_keys = project(whole_self, self_key).astype(low)
    self_values = project(whole_self, self_value).astype(low)
    self_mixed, self_logs = attention(self_queries, self_keys, self_values, latent_ids, latent_ids)
    after_self = after_cross + sum_rows(project_back(self_mixed, self_out))
    normed_mlp = layer_norm(after_self, ln_gain[3], ln_bias[3]).astype(low)
    whole_mlp = share_rows(normed_mlp)
    hidden = project(whole_mlp, up_proj)
    active = gelu_tanh(hidden).astype(low)
    grad_active = project(whole_grad_out, down_proj)
    gelu_value, gelu_pull = jax.vjp(gelu_tanh, hidden)
    grad_hidden = gelu_pull(grad_active)[0].astype(low)
    grad_normed = sum_rows(project_back(grad_hidden, up_proj))
    block_output = after_self + sum_rows(project_back(active, down_proj))
    down_grad = outer_sum(whole_grad_out, active).astype(low)
    up_grad = outer_sum(whole_mlp, grad_hidden).astype(low)
    grad_last = out_grad.astype(jnp.float32)
    norm_value, norm_pull = jax.vjp(layer_norm, after_self, ln_gain[3], ln_bias[3])
    grad_rows, gain_mlp, bias_mlp = norm_pull(grad_normed)
    grad_self = grad_last + grad_rows
    whole_grad = share_rows(grad_self.astype(low))
    self_out_grad = outer_sum(whole_grad, self_mixed).astype(low)
    grad_mixed = project(whole_grad, self_out).astype(low)
    query_grads, key_grads, value_grads = attention_back(
        self_queries, self_keys, self_values, self_logs, grad_mixed, latent_ids, latent_ids
    )
    self_grads = outer_sum(
        whole_self, jnp.concatenate([query_grads, key_grads, value_grads], axis=1)
    ).astype(low)
    grad_normed = sum_rows(
        project_back(query_grads, self_query)
        + project_back(key_grads, self_key)
        + project_back(value_grads, self_value)
    )
    norm_value, norm_pull = jax.vjp(layer_norm, after_cross, ln_gain[2], ln_bias[2])
    grad_rows, gain_self, bias_self = norm_pull(grad_normed)
    grad_cross = grad_self + grad_rows
    whole_grad = share_rows(grad_cross.astype(low))
    cross_out_grad = outer_sum(whole_grad, cross_mixed).astype(low)
    grad_mixed = project(whole_grad, cross_out).astype(low)
    query_grads, key_grads, value_grads = attention_back(
        cross_queries, cross_keys, cross_values, cross_logs, grad_mixed, latent_ids, input_ids
    )
    slot_grads = outer_sum(table_pick, query_grads)
    cross_query_grad = outer_sum(normed_table, slot_grads.astype(low)).astype(low)
    key_value_grads = jnp.concatenate([key_grads, value_grads], axis=1)
    cross_grads = outer_sum(whole_input, key_value_grads).astype(low)
    grad_input = sum_rows(
        project_back(key_grads, cross_key) + project_back(value_grads, cross_value)
    )
    norm_value, norm_pull = jax.vjp(layer_norm, input_rows, ln_gain[1], ln_bias[1])
    grad_input_rows, gain_input, bias_input = norm_pull(grad_input)

    axes = ("dp", "mp")
    table_terms = jnp.concatenate(
        [
            project_back(slot_grads.astype(low), cross_query),
            outer_sum(own_pick, grad_cross.astype(low)),
        ],
        axis=1,
    ).astype(low)
    width = table_terms.shape[1] // 2
    table_terms = lax.psum(table_terms, axes).astype(jnp.float32)
    norm_value, norm_pull = jax.vjp(layer_norm, table_rows, ln_gain[0], ln_bias[0])
    grad_rows, gain_latent, bias_latent = norm_pull(table_terms[:, :width])
    table_grad = table_terms[:, width:] + grad_rows
    small = lax.psum(
        jnp.stack([gain_input, gain_self, gain_mlp, bias_input, bias_self, bias_mlp]), axes
    )
    ln_gain_grad = jnp.concatenate([gain_latent[None], small[:3]])
    ln_bias_grad = jnp.concatenate([bias_latent[None], small[3:5]])

    def summed(pieces):
        whole = jnp.concatenate(pieces, axis=1) if len(pieces) > 1 else pieces[0]
        return lax.psum_scatter(whole, "dp", scatter_dimension=0, tiled=True).astype(jnp.float32)

    mlp_sum = summed([up_grad, down_grad])
    self_sum = summed([self_grads, self_out_grad])
    cross_sum = summed([cross_query_grad, cross_grads, cross_out_grad])
    up_width = up_grad.shape[1]
    heads_width = cross_query.shape[1]

    def column(whole, index):
        return whole[:, index * heads_width : (index + 1) * heads_width]

    return (
        block_output,
        grad_input_rows,
        table_grad,
        ln_gain_grad,
        ln_bias_grad,
        small[5],
        column(cross_sum, 0),
        column(cross_sum, 1),
        column(cross_sum, 2),
        column(cross_sum, 3),
        column(self_sum, 0),
        column(self_sum, 1),
        column(self_sum, 2),
        column(self_sum, 3),
        mlp_sum[:, :up_width],
        mlp_sum[:, up_width:],
    )


def solution(mesh):
    placed = (
        P(("dp", "mp"), None),
        P(),
        P("dp", None),
        P("dp", None),
        P(),
        P(),
        P(None, "mp"),
        P(None, "mp"),
        P(None, "mp"),
        P(None, "mp"),
        P(None, "mp"),
        P(None, "mp"),
        P(None, "mp"),
        P(None, "mp"),
        P(None, "mp"),
        P(None, "mp"),
        P(("dp", "mp"), None),
    )
    return jax.shard_map(
        body,
        mesh=mesh,
        in_specs=placed,
        out_specs=(
            P(("dp", "mp"), None),
            P(("dp", "mp"), None),
            P(),
            P(),
            P(),
            P(),
            P("dp", "mp"),
            P("dp", "mp"),
            P("dp", "mp"),
            P("dp", "mp"),
            P("dp", "mp"),
            P("dp", "mp"),
            P("dp", "mp"),
            P("dp", "mp"),
            P("dp", "mp"),
            P("dp", "mp"),
        ),
        check_vma=False,
    )
```

time: 1510 us -> 633 us (0.42)
  waiting for transfers between devices: 1170 us -> 252 us
  starting transfers between devices: 2.29 us -> 29 us
  local copies, waits for them, and re-layouts: 53.1 us -> 74.8 us
    reduce_scatter x17 -> x0, waiting for transfers between devices: 900 us -> none  [the longest x4 171 us: send_grads(): lax.psum_scatter(row_term(jnp.int32(0), local_count * lax.axis_size('mp')...]
    all_gather x7 -> x0, waiting for transfers between devices: 135 us -> none  [the longest x4 81 us: gather_rows(): return lax.all_gather(local_rows, 'mp', axis=0, tiled=True)]
    ppermute x0 -> x36, waiting for transfers between devices: none -> 131 us  [swap(): lax.ppermute(values, axis, [(i, i ^ bit) for i in range(lax.axis_size(axi...]
    ppermute x0 -> x36, starting transfers between devices: none -> 28.1 us  [swap(): lax.ppermute(values, axis, [(i, i ^ bit) for i in range(lax.axis_size(axi...]
    psum x1, waiting for transfers between devices: 135 us -> 110 us  [body(): table_terms = lax.psum(table_terms, axes).astype(jnp.float32)]
    dot_general x10 -> x9, matrix products: 35.9 us -> 23.6 us  [outer_sum(): lax.dot_general(left, right, (((0,), (0,)), ((), ())), preferred_element_...]
  transfers between devices with their start and end apart: 25 -> 40, of which waited for: 25 -> 20; matrix products, arithmetic and copies ran while one was open for 8% -> 14% of each run, Pallas kernels for 0% -> 0%
where the time goes in v1:
time: 633 us; the launch traced here: 626 us
  waiting for transfers between devices  252 us (40%)
  matrix products  154 us (24%)
  local copies, waits for them, and re-layouts  74.8 us (12%)
  other arithmetic  48.6 us (8%)
  blocking collectives  43.2 us (7%)
  starting transfers between devices  29 us (5%)
  between operations  17.4 us (3%)
  loops' own time  7.24 us (1%)
    ppermute x36, waiting for transfers between devices, swap(): lax.ppermute(values, axis, [(i, i ^ bit) for i in range(lax.axis_size(axi...  131 us
    psum x1, waiting for transfers between devices, body(): table_terms = lax.psum(table_terms, axes).astype(jnp.float32)  110 us
    psum x1, blocking collectives, body(): lax.psum(jnp.stack([gain_input, gain_self, gain_mlp, bias_input, bias_sel...  43.2 us
    dot_general x11, matrix products, project(): return jnp.dot(left, right, preferred_element_type=jnp.float32)  30.4 us
    unnamed x167, local copies, waits for them, and re-layouts  29.4 us
    ppermute x36, starting transfers between devices, swap(): lax.ppermute(values, axis, [(i, i ^ bit) for i in range(lax.axis_size(axi...  28.1 us
    dot_general x9, matrix products, outer_sum(): lax.dot_general(left, right, (((0,), (0,)), ((), ())), preferred_element_...  23.6 us
    dot_general x10, matrix products, project_back(): lax.dot_general(left, right, (((1,), (1,)), ((), ())), preferred_element_...  22.9 us
  transfers between devices with their start and end apart: 40, of which 20 were waited for; matrix products, arithmetic and copies ran while one was open for 14% of the time, Pallas kernels for 0%

profile of v1, /device:TPU:0, one launch (start us, length us, event | category | flops | bytes accessed | tf_op | source)
XLA Modules:
  0.0 626.3 jit_solution(14927736445263198143)
XLA Ops:
  12.6 2.1 fusion.68
  14.7 2.9 collective-permute-start.1
  22.6 7.3 %collective-permute-done.1 = bf16[256,1024]{1,0:T(8,128)(2,1)} collective-permute-done((bf16[256,1024]{1,0:T(8,128)(2,1)}, bf16[256,1024]{1,0:T(8,128)(2,1)}, u32[]{:S(2)}, u32[]{:S(2)}) %collective-permute-start.1) | collective-permute-done | bytes 524320 | tf_op jit(solution)/shard_map/ppermute | solution.py:49
  33.0 3.1 convolution_convert_fusion.15
  37.5 3.1 convolution_convert_fusion.14
  41.4 14.9 %while.54 = (s32[]{:T(128)}, bf16[2,512,256]{2,1,0:T(8,128)(2,1)}, f32[2,2,512,1]{2,1,3,0:T(2,128)S(1)}, s32[2]{0:T(128)S(1)}, s32[1024]{0:T(1024)S(1)}, /*index...) while((s32[]{:T(128)}, bf16[2,512,256]{2,1,0:T(8,128)(2,1)}, ...), condition=%wide.region_8.9_spmd, body=%wide.region_5.8_spmd.sunk | while | flops 548928512 | bytes 19966688 | solution.py:107
  63.4 11.5 %collective-permute-done.5 = bf16[256,1024]{1,0:T(8,128)(2,1)S(1)} collective-permute-done((bf16[256,1024]{1,0:T(8,128)(2,1)S(1)}, bf16[256,1024]{1,0:T(8,128)(2,1)S(1)}, u32[]{:S(2)}, u32[]{:S(2)}) %collective-permute-start.5) | collective-permute-done | bytes 524320 | tf_op jit(solution)/shard_map/ppermute | solution.py:49
  78.3 12.0 %collective-permute-done.7 = bf16[256,1024]{1,0:T(8,128)(2,1)} collective-permute-done((bf16[256,1024]{1,0:T(8,128)(2,1)}, bf16[256,1024]{1,0:T(8,128)(2,1)}, u32[]{:S(2)}, u32[]{:S(2)}) %collective-permute-start.7) | collective-permute-done | bytes 524320 | tf_op jit(solution)/shard_map/ppermute | solution.py:49
  90.2 2.2 collective-permute-done.8
  92.5 3.3 convolution_convert_fusion.12
  97.8 3.2 convolution_convert_fusion.13
  103.1 3.2 convolution_convert_fusion.11
  107.2 20.6 %while.55 = (s32[]{:T(128)}, bf16[2,512,256]{2,1,0:T(8,128)(2,1)}, f32[2,2,512,1]{2,1,3,0:T(2,128)S(1)}, s32[2]{0:T(128)S(1)}, s32[1024]{0:T(1024)S(1)}, /*index...) while((s32[]{:T(128)}, bf16[2,512,256]{2,1,0:T(8,128)(2,1)}, ...), condition=%wide.region_14.15_spmd, body=%wide.region_11.14_spmd.sunk | while | flops 548928512 | bytes 19966680 | solution.py:107
  110.4 2.3 fusion.258
  120.4 2.3 fusion.258
  134.1 12.7 %collective-permute-done.11 = bf16[256,1024]{1,0:T(8,128)(2,1)S(1)} collective-permute-done((bf16[256,1024]{1,0:T(8,128)(2,1)S(1)}, bf16[256,1024]{1,0:T(8,128)(2,1)S(1)}, u32[]{:S(2)}, u32[]{:S(2)}) %collective-permute-start.11) | collective-permute-done | bytes 524320 | tf_op jit(solution)/shard_map/ppermute | solution.py:49
  149.5 8.6 %collective-permute-done.19 = bf16[256,1024]{1,0:T(8,128)(2,1)S(1)} collective-permute-done((bf16[256,1024]{1,0:T(8,128)(2,1)S(1)}, bf16[256,1024]{1,0:T(8,128)(2,1)S(1)}, u32[]{:S(2)}, u32[]{:S(2)}) %collective-permute-start.19) | collective-permute-done | bytes 524320 | tf_op jit(solution)/shard_map/ppermute | solution.py:49
  158.6 9.9 %collective-permute-done.13 = bf16[256,1024]{1,0:T(8,128)(2,1)S(1)} collective-permute-done((bf16[256,1024]{1,0:T(8,128)(2,1)S(1)}, bf16[256,1024]{1,0:T(8,128)(2,1)S(1)}, u32[]{:S(2)}, u32[]{:S(2)}) %collective-permute-start.13) | collective-permute-done | bytes 524320 | tf_op jit(solution)/shard_map/ppermute | solution.py:49
  170.4 2.3 fusion.98
  172.8 5.6 fusion.47
  178.5 2.4 fusion.143
  181.2 2.6 fusion.144
  187.8 11.6 %collective-permute-done.23 = bf16[256,1024]{1,0:T(8,128)(2,1)S(1)} collective-permute-done((bf16[256,1024]{1,0:T(8,128)(2,1)S(1)}, bf16[256,1024]{1,0:T(8,128)(2,1)S(1)}, u32[]{:S(2)}, u32[]{:S(2)}) %collective-permute-start.23) | collective-permute-done | bytes 524320 | tf_op jit(solution)/shard_map/ppermute | solution.py:49
  200.5 9.6 %collective-permute-done.17 = bf16[256,1024]{1,0:T(8,128)(2,1)S(1)} collective-permute-done((bf16[256,1024]{1,0:T(8,128)(2,1)S(1)}, bf16[256,1024]{1,0:T(8,128)(2,1)S(1)}, u32[]{:S(2)}, u32[]{:S(2)}) %collective-permute-start.17) | collective-permute-done | bytes 524320 | tf_op jit(solution)/shard_map/ppermute | solution.py:49
  213.6 11.7 %collective-permute-done.25 = bf16[256,1024]{1,0:T(8,128)(2,1)S(1)} collective-permute-done((bf16[256,1024]{1,0:T(8,128)(2,1)S(1)}, bf16[256,1024]{1,0:T(8,128)(2,1)S(1)}, u32[]{:S(2)}, u32[]{:S(2)}) %collective-permute-start.25) | collective-permute-done | bytes 524320 | tf_op jit(solution)/shard_map/ppermute | solution.py:49
  230.1 45.7 %while.56 = (s32[]{:T(128)}, f32[1024,2,128]{0,2,1:T(8,128)}, f32[1024,2,128]{0,2,1:T(8,128)}, bf16[2,512,256]{2,1,0:T(8,128)(2,1)}, s32[2]{0:T(128)S(1)}, /*ind...) while((s32[]{:T(128)}, f32[1024,2,128]{0,2,1:T(8,128)}, ...), condition=%wide.region_21.22_spmd.clone, body=%wide.region_19.21_spmd.clone.sunk | while | flops 1360002048 | bytes 85236632 | solution.py:154
  232.7 3.8 fusion.270
  237.1 4.2 multiply_reduce_fusion.10
  242.7 2.6 convolution_multiply_fusion.6
  249.7 2.4 fusion.272
  254.5 3.8 fusion.270
  259.0 4.2 multiply_reduce_fusion.10
  264.6 2.6 convolution_multiply_fusion.6
  269.0 2.8 fusion.271
  271.8 3.7 fusion.272
  286.0 12.2 %collective-permute-done.29 = bf16[256,1024]{1,0:T(8,128)(2,1)S(1)} collective-permute-done((bf16[256,1024]{1,0:T(8,128)(2,1)S(1)}, bf16[256,1024]{1,0:T(8,128)(2,1)S(1)}, u32[]{:S(2)}, u32[]{:S(2)}) %collective-permute-start.29) | collective-permute-done | bytes 524320 | tf_op jit(solution)/shard_map/ppermute | solution.py:49
  303.9 9.9 %collective-permute-done.31 = bf16[256,1024]{1,0:T(8,128)(2,1)} collective-permute-done((bf16[256,1024]{1,0:T(8,128)(2,1)}, bf16[256,1024]{1,0:T(8,128)(2,1)}, u32[]{:S(2)}, u32[]{:S(2)}) %collective-permute-start.31) | collective-permute-done | bytes 524320 | tf_op jit(solution)/shard_map/ppermute | solution.py:49
  313.8 4.7 convolution_convert_fusion.2
  318.5 2.3 convolution_convert_fusion.8
  320.8 2.3 convolution_convert_fusion.9
  324.0 45.4 %while.57 = (s32[]{:T(128)}, f32[1024,2,128]{0,2,1:T(8,128)}, f32[1024,2,128]{0,2,1:T(8,128)}, bf16[2,512,256]{2,1,0:T(8,128)(2,1)}, s32[2]{0:T(128)S(1)}, /*ind...) while((s32[]{:T(128)}, f32[1024,2,128]{0,2,1:T(8,128)}, ...), condition=%wide.region_26.27_spmd.clone, body=%wide.region_24.26_spmd.clone.sunk | while | flops 1360002048 | bytes 85236640 | solution.py:154
  326.6 3.8 fusion.283
  331.1 4.2 multiply_reduce_fusion.11
  336.7 2.6 convolution_multiply_fusion.7
  343.6 2.4 fusion.285
  348.4 3.8 fusion.283
  352.8 4.2 multiply_reduce_fusion.11
  358.4 2.6 convolution_multiply_fusion.7
  362.8 2.8 fusion.284
  365.7 3.7 fusion.285
  377.1 2.6 copy.180
  380.4 4.6 convolution_convert_fusion.1
  385.0 2.9 convolution_convert_fusion
  387.9 2.4 pad_maximum_fusion
  390.3 6.5 %copy.182 = bf16[1024,2048]{1,0:T(8,128)(2,1)} copy(bf16[1024,2048]{0,1:T(8,128)(2,1)} %pad_maximum_fusion) | data formatting | bytes 8388608
  400.2 2.9 convolution_convert_fusion.3
  405.3 2.6 copy.178
  407.9 4.0 fusion.151
  411.9 5.2 fusion.146
  418.7 109.9 %all-reduce.2.cloned.1.call-done = bf16[256,2048]{1,0:T(8,128)(2,1)} async-done(((bf16[256,2048]{1,0:T(8,128)(2,1)}), bf16[256,2048]{1,0:T(8,128)(2,1)}) %all-reduce.2.cloned.1.call-update) | async-done | bytes 1048592 | tf_op jit(solution)/shard_map/psum | solution.py:284
  532.3 5.7 collective-permute-start.35
  539.9 5.2 collective-permute-done.35
  547.3 43.2 %psum.15 = f32[6,1024]{1,0:T(8,128)S(1)} all-reduce(f32[6,1024]{1,0:T(8,128)S(1)} %stack.2), channel_id=1, replica_groups=mesh['dp'=8,'mp'=4] {'dp','mp'}, use_global_device_ids=true, to_apply=%region_39.40 | all-reduce | flops 6144 | bytes 49152 | tf_op jit(solution)/shard_map/psum | solution.py:288
  603.1 11.2 %reduce-scatter.10.cloned.1.call-done = bf16[128,1024]{1,0:T(8,128)(2,1)} async-done(((bf16[1024,1024]{1,0:T(8,128)(2,1)}), bf16[128,1024]{1,0:T(8,128)(2,1)}) %reduce-scatter.10.cloned.1.call-update) | async-done | bytes 262160
  (484 shorter events, 165.5 us)
Async XLA Ops:
  8.0 162.4 %copy-start = (bf16[1024,1024]{1,0:T(8,128)(2,1)S(1)}, bf16[1024,1024]{1,0:T(8,128)(2,1)}, u32[]{:S(2)}) copy-start(bf16[1024,1024]{1,0:T(8,128)(2,1)} %param.39) | copy-start | bytes 6291460
  8.0 25.0 %copy-start.35 = (bf16[1024,256]{1,0:T(8,128)(2,1)S(1)}, bf16[1024,256]{1,0:T(8,128)(2,1)}, u32[]{:S(2)}) copy-start(bf16[1024,256]{1,0:T(8,128)(2,1)} %param.32) | copy-start | bytes 1572868
  8.0 520.5 %all-reduce.2.cloned.1.call-start = ((), (), s32[]{:S(2)}) async-start(), calls=%async_computation.3 | async-start | bytes 2097152 | tf_op jit(solution)/shard_map/psum | solution.py:284
  9.1 23.9 %copy-start.51 = (f32[1,1024]{1,0:T(1,128)}, f32[1,1024]{1,0:T(1,128)S(1)}, u32[]{:S(2)}) copy-start(f32[1,1024]{1,0:T(1,128)S(1)} %get-tuple-element.680) | copy-start | bytes 12292
  10.0 23.0 %copy-start.71 = (f32[1,1024]{1,0:T(1,128)}, f32[1,1024]{1,0:T(1,128)S(1)}, u32[]{:S(2)}) copy-start(f32[1,1024]{1,0:T(1,128)S(1)} %get-tuple-element.684) | copy-start | bytes 12292
  11.2 21.8 %copy-start.53 = (f32[256]{0:T(256)}, f32[256]{0:T(256)S(1)}, u32[]{:S(2)}) copy-start(f32[256]{0:T(256)S(1)} %broadcast_multiply_fusion.2) | copy-start | bytes 3076
  12.5 23.6 %copy-start.65 = (f32[256]{0:T(256)}, f32[256]{0:T(256)S(1)}, u32[]{:S(2)}) copy-start(f32[256]{0:T(256)S(1)} %fusion.75) | copy-start | bytes 3076
  12.5 20.4 %copy-start.57 = (f32[256]{0:T(256)}, f32[256]{0:T(256)S(1)}, u32[]{:S(2)}) copy-start(f32[256]{0:T(256)S(1)} %fusion.103) | copy-start | bytes 3076
  14.7 15.2 %collective-permute-start.1 = (bf16[256,1024]{1,0:T(8,128)(2,1)}, bf16[256,1024]{1,0:T(8,128)(2,1)}, u32[]{:S(2)}, u32[]{:S(2)}) collective-permute-start(bf16[256,1024]{1,0:T(8,128)(2,1)} %fusion.68), channel_id=1, source_target_pairs={{0,2},{1,3},{2,0},{3,1},{4,6},{5,7},{6,4},{7,5},{8,10},{9,11},{10,... | collective-permute-start | bytes 1572872 | tf_op jit(solution)/shard_map/ppermute | solution.py:49
  17.6 15.4 %collective-permute-start = (bf16[256,1024]{1,0:T(8,128)(2,1)}, bf16[256,1024]{1,0:T(8,128)(2,1)}, u32[]{:S(2)}, u32[]{:S(2)}) collective-permute-start(bf16[256,1024]{1,0:T(8,128)(2,1)} %fusion.68), channel_id=1, source_target_pairs={{0,1},{1,0},{2,3},{3,2},{4,5},{5,4},{6,7},{7,6},{8,9},{9,8},{10,11... | collective-permute-start | bytes 1572872 | tf_op jit(solution)/shard_map/ppermute | solution.py:49
  22.6 39.9 %copy-start.61 = (s32[1024]{0:T(1024)}, s32[1024]{0:T(1024)S(1)}, u32[]{:S(2)}) copy-start(s32[1024]{0:T(1024)S(1)} %add_subtract_fusion) | copy-start | bytes 12292
  29.9 3.1 collective-permute-start.2
  58.4 2.1 collective-permute-start.4
  58.9 4.1 collective-permute-start.3
  60.6 14.3 %collective-permute-start.5 = (bf16[256,1024]{1,0:T(8,128)(2,1)S(1)}, bf16[256,1024]{1,0:T(8,128)(2,1)S(1)}, u32[]{:S(2)}, u32[]{:S(2)}) collective-permute-start(bf16[256,1024]{1,0:T(8,128)(2,1)S(1)} %fusion.89), channel_id=1, source_target_pairs={{0,2},{1,3},{2,0},{3,1},{4,6},{5,7},{6,4},{7,5},{8,10},{9,11},{10,... | collective-permute-start | bytes 1572872 | tf_op jit(solution)/shard_map/ppermute | solution.py:49
  75.2 71.7 %copy-start.7 = (f32[256,1024]{1,0:T(8,128)}, f32[256,1024]{1,0:T(8,128)S(1)}, u32[]{:S(2)}) copy-start(f32[256,1024]{1,0:T(8,128)S(1)} %get-tuple-element.646) | copy-start | bytes 3145732
  75.5 20.3 %copy-start.69 = (f32[256]{0:T(256)}, f32[256]{0:T(256)S(1)}, u32[]{:S(2)}) copy-start(f32[256]{0:T(256)S(1)} %multiply_reduce_fusion.7) | copy-start | bytes 3076
  76.5 13.7 %collective-permute-start.7 = (bf16[256,1024]{1,0:T(8,128)(2,1)}, bf16[256,1024]{1,0:T(8,128)(2,1)}, u32[]{:S(2)}, u32[]{:S(2)}) collective-permute-start(bf16[256,1024]{1,0:T(8,128)(2,1)} %add_convert_fusion.2), channel_id=1, source_target_pairs={{0,2},{1,3},{2,0},{3,1},{4,6},{5,7},{6,4},{7,5},{8,10},{9,11},{10,... | collective-permute-start | bytes 1572872 | tf_op jit(solution)/shard_map/ppermute | solution.py:49
  78.3 12.0 %collective-permute-start.6 = (bf16[256,1024]{1,0:T(8,128)(2,1)}, bf16[256,1024]{1,0:T(8,128)(2,1)}, u32[]{:S(2)}, u32[]{:S(2)}) collective-permute-start(bf16[256,1024]{1,0:T(8,128)(2,1)} %add_convert_fusion.2), channel_id=1, source_target_pairs={{0,1},{1,0},{2,3},{3,2},{4,5},{5,4},{6,7},{7,6},{8,9},{9,8},{10,11... | collective-permute-start | bytes 1572872 | tf_op jit(solution)/shard_map/ppermute | solution.py:49
  90.2 2.3 collective-permute-start.8
  129.9 2.0 collective-permute-start.10
  130.1 4.0 collective-permute-start.9
  132.0 14.8 %collective-permute-start.11 = (bf16[256,1024]{1,0:T(8,128)(2,1)S(1)}, bf16[256,1024]{1,0:T(8,128)(2,1)S(1)}, u32[]{:S(2)}, u32[]{:S(2)}) collective-permute-start(bf16[256,1024]{1,0:T(8,128)(2,1)S(1)} %fusion.86), channel_id=1, source_target_pairs={{0,2},{1,3},{2,0},{3,1},{4,6},{5,7},{6,4},{7,5},{8,10},{9,11},{10,... | collective-permute-start | bytes 1572872 | tf_op jit(solution)/shard_map/ppermute | solution.py:49
  133.8 24.3 %collective-permute-start.19 = (bf16[256,1024]{1,0:T(8,128)(2,1)S(1)}, bf16[256,1024]{1,0:T(8,128)(2,1)S(1)}, u32[]{:S(2)}, u32[]{:S(2)}) collective-permute-start(bf16[256,1024]{1,0:T(8,128)(2,1)S(1)} %copy-done.19), channel_id=1, source_target_pairs={{0,2},{1,3},{2,0},{3,1},{4,6},{5,7},{6,4},{7,5},{8,10},{9,11},{10,... | collective-permute-start | bytes 1572872 | tf_op jit(solution)/shard_map/ppermute | solution.py:49
  147.7 25.1 %copy-start.38 = (bf16[256,1024]{1,0:T(8,128)(2,1)}, bf16[256,1024]{1,0:T(8,128)(2,1)S(1)}, u32[]{:S(2)}) copy-start(bf16[256,1024]{1,0:T(8,128)(2,1)S(1)} %add_convert_fusion.1) | copy-start | bytes 1572868
  147.7 20.8 %collective-permute-start.13 = (bf16[256,1024]{1,0:T(8,128)(2,1)S(1)}, bf16[256,1024]{1,0:T(8,128)(2,1)S(1)}, u32[]{:S(2)}, u32[]{:S(2)}) collective-permute-start(bf16[256,1024]{1,0:T(8,128)(2,1)S(1)} %add_convert_fusion.1), channel_id=1, source_target_pairs={{0,2},{1,3},{2,0},{3,1},{4,6},{5,7},{6,4},{7,5},{8,10},{9,11},{10,... | collective-permute-start | bytes 1572872 | tf_op jit(solution)/shard_map/ppermute | solution.py:49
  149.5 19.0 %collective-permute-start.18 = (bf16[256,1024]{1,0:T(8,128)(2,1)S(1)}, bf16[256,1024]{1,0:T(8,128)(2,1)S(1)}, u32[]{:S(2)}, u32[]{:S(2)}) collective-permute-start(bf16[256,1024]{1,0:T(8,128)(2,1)S(1)} %copy-done.19), channel_id=1, source_target_pairs={{0,1},{1,0},{2,3},{3,2},{4,5},{5,4},{6,7},{7,6},{8,9},{9,8},{10,11... | collective-permute-start | bytes 1572872 | tf_op jit(solution)/shard_map/ppermute | solution.py:49
  158.1 10.6 %collective-permute-start.20 = (bf16[256,1024]{1,0:T(8,128)(2,1)S(1)}, bf16[256,1024]{1,0:T(8,128)(2,1)S(1)}, u32[]{:S(2)}, u32[]{:S(2)}) collective-permute-start(bf16[256,1024]{1,0:T(8,128)(2,1)S(1)} %collective-permute-done.19), channel_id=1, source_target_pairs={{0,1},{1,0},{2,3},{3,2},{4,5},{5,4},{6,7},{7,6},{8,9},{9,8},{10,11... | collective-permute-start | bytes 1572872 | tf_op jit(solution)/shard_map/ppermute | solution.py:49
  158.1 10.7 %collective-permute-start.12 = (bf16[256,1024]{1,0:T(8,128)(2,1)S(1)}, bf16[256,1024]{1,0:T(8,128)(2,1)S(1)}, u32[]{:S(2)}, u32[]{:S(2)}) collective-permute-start(bf16[256,1024]{1,0:T(8,128)(2,1)S(1)} %add_convert_fusion.1), channel_id=1, source_target_pairs={{0,1},{1,0},{2,3},{3,2},{4,5},{5,4},{6,7},{7,6},{8,9},{9,8},{10,11... | collective-permute-start | bytes 1572872 | tf_op jit(solution)/shard_map/ppermute | solution.py:49
  168.5 1.9 collective-permute-start.14
  181.0 3.5 collective-permute-start.22
  183.9 2.6 collective-permute-start.16
  184.3 3.5 collective-permute-start.21
  184.6 14.8 %collective-permute-start.23 = (bf16[256,1024]{1,0:T(8,128)(2,1)S(1)}, bf16[256,1024]{1,0:T(8,128)(2,1)S(1)}, u32[]{:S(2)}, u32[]{:S(2)}) collective-permute-start(bf16[256,1024]{1,0:T(8,128)(2,1)S(1)} %fusion.81), channel_id=1, source_target_pairs={{0,2},{1,3},{2,0},{3,1},{4,6},{5,7},{6,4},{7,5},{8,10},{9,11},{10,... | collective-permute-start | bytes 1572872 | tf_op jit(solution)/shard_map/ppermute | solution.py:49
  186.4 14.1 %collective-permute-start.15 = (bf16[256,1024]{1,0:T(8,128)(2,1)S(1)}, bf16[256,1024]{1,0:T(8,128)(2,1)S(1)}, u32[]{:S(2)}, u32[]{:S(2)}) collective-permute-start(bf16[256,1024]{1,0:T(8,128)(2,1)S(1)} %get-tuple-element.661), channel_id=1, source_target_pairs={{0,1},{1,0},{2,3},{3,2},{4,5},{5,4},{6,7},{7,6},{8,9},{9,8},{10,11... | collective-permute-start | bytes 1572872 | tf_op jit(solution)/shard_map/ppermute | solution.py:49
  186.7 23.5 %collective-permute-start.17 = (bf16[256,1024]{1,0:T(8,128)(2,1)S(1)}, bf16[256,1024]{1,0:T(8,128)(2,1)S(1)}, u32[]{:S(2)}, u32[]{:S(2)}) collective-permute-start(bf16[256,1024]{1,0:T(8,128)(2,1)S(1)} %fusion.83), channel_id=1, source_target_pairs={{0,2},{1,3},{2,0},{3,1},{4,6},{5,7},{6,4},{7,5},{8,10},{9,11},{10,... | collective-permute-start | bytes 1572872 | tf_op jit(solution)/shard_map/ppermute | solution.py:49
  210.1 17.2 %copy-start.31 = (bf16[1024,256]{1,0:T(8,128)(2,1)S(1)}, bf16[1024,256]{1,0:T(8,128)(2,1)}, u32[]{:S(2)}) copy-start(bf16[1024,256]{1,0:T(8,128)(2,1)} %param.38) | copy-start | bytes 1572868
  211.8 17.4 %copy-start.41 = (bf16[256,1024]{1,0:T(8,128)(2,1)}, bf16[256,1024]{1,0:T(8,128)(2,1)S(1)}, u32[]{:S(2)}) copy-start(bf16[256,1024]{1,0:T(8,128)(2,1)S(1)} %fusion.95) | copy-start | bytes 1572868
  211.8 13.5 %collective-permute-start.25 = (bf16[256,1024]{1,0:T(8,128)(2,1)S(1)}, bf16[256,1024]{1,0:T(8,128)(2,1)S(1)}, u32[]{:S(2)}, u32[]{:S(2)}) collective-permute-start(bf16[256,1024]{1,0:T(8,128)(2,1)S(1)} %fusion.95), channel_id=1, source_target_pairs={{0,2},{1,3},{2,0},{3,1},{4,6},{5,7},{6,4},{7,5},{8,10},{9,11},{10,... | collective-permute-start | bytes 1572872 | tf_op jit(solution)/shard_map/ppermute | solution.py:49
  213.6 13.2 %collective-permute-start.24 = (bf16[256,1024]{1,0:T(8,128)(2,1)S(1)}, bf16[256,1024]{1,0:T(8,128)(2,1)}, u32[]{:S(2)}, u32[]{:S(2)}) collective-permute-start(bf16[256,1024]{1,0:T(8,128)(2,1)S(1)} %fusion.95), channel_id=1, source_target_pairs={{0,1},{1,0},{2,3},{3,2},{4,5},{5,4},{6,7},{7,6},{8,9},{9,8},{10,11... | collective-permute-start | bytes 1572872 | tf_op jit(solution)/shard_map/ppermute | solution.py:49
  225.2 2.0 collective-permute-start.26
  281.9 16.3 %copy-start.8 = (f32[256,1024]{1,0:T(8,128)S(1)}, f32[256,1024]{1,0:T(8,128)}, u32[]{:S(2)}) copy-start(f32[256,1024]{1,0:T(8,128)} %copy-done.7) | copy-start | bytes 3145732
  282.0 16.8 %copy-start.70 = (f32[256]{0:T(256)S(1)}, f32[256]{0:T(256)}, u32[]{:S(2)}) copy-start(f32[256]{0:T(256)} %copy-done.69) | copy-start | bytes 3076
  282.0 2.0 collective-permute-start.28
  282.2 3.7 collective-permute-start.27
  284.2 15.0 %copy-start.18 = (f32[256,1024]{1,0:T(8,128)S(1)}, f32[256,1024]{1,0:T(8,128)}, u32[]{:S(2)}) copy-start(f32[256,1024]{1,0:T(8,128)} %copy-done.17) | copy-start | bytes 3145732
  284.2 15.0 %copy-start.20 = (bf16[256,1024]{1,0:T(8,128)(2,1)S(1)}, bf16[256,1024]{1,0:T(8,128)(2,1)}, u32[]{:S(2)}) copy-start(bf16[256,1024]{1,0:T(8,128)(2,1)} %param.41) | copy-start | bytes 1572868
  284.2 14.0 %collective-permute-start.29 = (bf16[256,1024]{1,0:T(8,128)(2,1)S(1)}, bf16[256,1024]{1,0:T(8,128)(2,1)S(1)}, u32[]{:S(2)}, u32[]{:S(2)}) collective-permute-start(bf16[256,1024]{1,0:T(8,128)(2,1)S(1)} %fusion.79), channel_id=1, source_target_pairs={{0,2},{1,3},{2,0},{3,1},{4,6},{5,7},{6,4},{7,5},{8,10},{9,11},{10,... | collective-permute-start | bytes 1572872 | tf_op jit(solution)/shard_map/ppermute | solution.py:49
  300.4 13.5 %collective-permute-start.31 = (bf16[256,1024]{1,0:T(8,128)(2,1)}, bf16[256,1024]{1,0:T(8,128)(2,1)}, u32[]{:S(2)}, u32[]{:S(2)}) collective-permute-start(bf16[256,1024]{1,0:T(8,128)(2,1)} %add_convert_fusion), channel_id=1, source_target_pairs={{0,2},{1,3},{2,0},{3,1},{4,6},{5,7},{6,4},{7,5},{8,10},{9,11},{10,... | collective-permute-start | bytes 1572872 | tf_op jit(solution)/shard_map/ppermute | solution.py:49
  303.8 17.0 %copy-start.32 = (bf16[1024,256]{1,0:T(8,128)(2,1)S(1)}, bf16[1024,256]{1,0:T(8,128)(2,1)}, u32[]{:S(2)}) copy-start(bf16[1024,256]{1,0:T(8,128)(2,1)} %param.34) | copy-start | bytes 1572868
  303.8 16.9 %collective-permute-start.30 = (bf16[256,1024]{1,0:T(8,128)(2,1)}, bf16[256,1024]{1,0:T(8,128)(2,1)S(1)}, u32[]{:S(2)}, u32[]{:S(2)}) collective-permute-start(bf16[256,1024]{1,0:T(8,128)(2,1)} %add_convert_fusion), channel_id=1, source_target_pairs={{0,1},{1,0},{2,3},{3,2},{4,5},{5,4},{6,7},{7,6},{8,9},{9,8},{10,11... | collective-permute-start | bytes 1572872 | tf_op jit(solution)/shard_map/ppermute | solution.py:49
  313.8 7.0 %collective-permute-start.32 = (bf16[256,1024]{1,0:T(8,128)(2,1)}, bf16[256,1024]{1,0:T(8,128)(2,1)S(1)}, u32[]{:S(2)}, u32[]{:S(2)}) collective-permute-start(bf16[256,1024]{1,0:T(8,128)(2,1)} %collective-permute-done.31), channel_id=1, source_target_pairs={{0,1},{1,0},{2,3},{3,2},{4,5},{5,4},{6,7},{7,6},{8,9},{9,8},{10,11... | collective-permute-start | bytes 1572872 | tf_op jit(solution)/shard_map/ppermute | solution.py:49
  324.0 45.5 %copy-start.62 = (s32[1024]{0:T(1024)S(1)}, s32[1024]{0:T(1024)}, u32[]{:S(2)}) copy-start(s32[1024]{0:T(1024)} %copy-done.61) | copy-start | bytes 12292
  374.8 219.0 %reduce-scatter.12.cloned.1.call-start = ((), (), s32[]{:S(2)}) async-start(), calls=%async_computation.5 | async-start | bytes 2359296
  379.8 218.1 %reduce-scatter.14.cloned.1.call-start = ((), (), s32[]{:S(2)}) async-start(), calls=%async_computation.6 | async-start | bytes 4718592
  396.9 217.5 %reduce-scatter.10.cloned.1.call-start = ((), (), s32[]{:S(2)}) async-start(), calls=%async_computation.4 | async-start | bytes 2359296
  417.1 113.4 %copy-start.68 = (f32[256]{0:T(256)S(1)}, f32[256]{0:T(256)}, u32[]{:S(2)}) copy-start(f32[256]{0:T(256)} %copy-done.67) | copy-start | bytes 3076
  418.2 112.4 %collective-permute-start.34 = (bf16[256,1024]{1,0:T(8,128)(2,1)}, bf16[256,1024]{1,0:T(8,128)(2,1)}, u32[]{:S(2)}, u32[]{:S(2)}) collective-permute-start(bf16[256,1024]{1,0:T(8,128)(2,1)} %get-tuple-element.656), channel_id=1, source_target_pairs={{0,1},{1,0},{2,3},{3,2},{4,5},{5,4},{6,7},{7,6},{8,9},{9,8},{10,11... | collective-permute-start | bytes 1572872 | tf_op jit(solution)/shard_map/ppermute | solution.py:49
  418.6 121.3 %collective-permute-start.33 = (bf16[256,1024]{1,0:T(8,128)(2,1)}, bf16[256,1024]{1,0:T(8,128)(2,1)}, u32[]{:S(2)}, u32[]{:S(2)}) collective-permute-start(bf16[256,1024]{1,0:T(8,128)(2,1)} %get-tuple-element.655), channel_id=1, source_target_pairs={{0,1},{1,0},{2,3},{3,2},{4,5},{5,4},{6,7},{7,6},{8,9},{9,8},{10,11... | collective-permute-start | bytes 1572872 | tf_op jit(solution)/shard_map/ppermute | solution.py:49
  530.2 15.0 %copy-start.15 = (bf16[256,1024]{1,0:T(8,128)(2,1)S(1)}, bf16[256,1024]{1,0:T(8,128)(2,1)}, u32[]{:S(2)}) copy-start(bf16[256,1024]{1,0:T(8,128)(2,1)} %param.25) | copy-start | bytes 1572868
  530.2 15.0 %copy-start.48 = (f32[1,1024]{1,0:T(1,128)S(1)}, f32[1,1024]{1,0:T(1,128)}, u32[]{:S(2)}) copy-start(f32[1,1024]{1,0:T(1,128)} %copy-done.47) | copy-start | bytes 12292
  530.2 14.9 %copy-start.54 = (f32[256]{0:T(256)S(1)}, f32[256]{0:T(256)}, u32[]{:S(2)}) copy-start(f32[256]{0:T(256)} %copy-done.53) | copy-start | bytes 3076
  532.3 12.8 %collective-permute-start.35 = (bf16[256,1024]{1,0:T(8,128)(2,1)S(1)}, bf16[256,1024]{1,0:T(8,128)(2,1)S(1)}, u32[]{:S(2)}, u32[]{:S(2)}) collective-permute-start(bf16[256,1024]{1,0:T(8,128)(2,1)S(1)} %fusion.77), channel_id=1, source_target_pairs={{0,2},{1,3},{2,0},{3,1},{4,6},{5,7},{6,4},{7,5},{8,10},{9,11},{10,... | collective-permute-start | bytes 1572872 | tf_op jit(solution)/shard_map/ppermute | solution.py:49
  596.4 22.2 %copy-start.1 = (bf16[1024,1024]{1,0:T(8,128)(2,1)S(1)}, bf16[1024,1024]{1,0:T(8,128)(2,1)}, u32[]{:S(2)}) copy-start(bf16[1024,1024]{1,0:T(8,128)(2,1)} %param.39) | copy-start | bytes 6291460
  (77 other events, 396.0 us)
Sparse Core Ops, SparseCore 0:
  374.9 153.6 all-reduce.1
Sparse Core Ops, SparseCore 1:
  379.9 69.9 reduce-scatter.11
  453.8 89.0 reduce-scatter.13
  546.3 68.0 reduce-scatter.9
